TPU v7x, 128 devices: a whole 4x4x4 slice. The times are simulated.
128 devices in a mesh: rep: 16 (over y_hi, x, core), shard: 8 (over y_lo, z).
Axes of the slice: x: 4, y: 4 (y_hi: 2, y_lo: 2; y = y_hi * 2 + y_lo), z: 4, core: 2. Of those that a mesh axis runs over, the one named last changes fastest.
Arguments:
- tokens: bfloat16 [16384, 1600], P(('rep', 'shard')), may hold values from -6 to 6
- lengths: int32 [16, 4], P('rep'), may hold values from 1 to 1021, as said below
- ln1_gain: bfloat16 [1600], P('shard'), may hold values from 0.25 to 1.75
- ln1_bias: bfloat16 [1600], P('shard'), may hold values from -3 to 3
- qkv_weight: bfloat16 [1600, 4800], P('shard'), may hold values from -0.15625 to 0.15625
- q_bias: bfloat16 [1600], P('shard'), may hold values from -3 to 3
- v_bias: bfloat16 [1600], P('shard'), may hold values from -3 to 3
- out_weight: bfloat16 [1600, 1600], P('shard'), may hold values from -0.625 to 0.625
- out_bias: bfloat16 [1600], P('shard'), may hold values from -2 to 2
- ln2_gain: bfloat16 [1600], P('shard'), may hold values from 0.25 to 1.75
- ln2_bias: bfloat16 [1600], P('shard'), may hold values from -3 to 3
- fc_weight: bfloat16 [1600, 6400], P('shard'), may hold values from -0.15625 to 0.15625
- fc_bias: bfloat16 [6400], P('shard'), may hold values from -3 to 3
- proj_weight: bfloat16 [6400, 1600], P('shard'), may hold values from -0.078125 to 0.078125
- proj_bias: bfloat16 [1600], P('shard'), may hold values from -2 to 2
- cotangent: bfloat16 [16384, 1600], P(('rep', 'shard')), may hold values from -6 to 6
Outputs:
- output: bfloat16 [16384, 1600], P(('rep', 'shard'))
- input_grad: float32 [16384, 1600], P(('rep', 'shard'))
- grad_ln1_gain: float32 [1600], P('shard')
- grad_ln1_bias: float32 [1600], P('shard')
- grad_qkv_weight: float32 [1600, 4800], P('shard')
- grad_q_bias: float32 [1600], P('shard')
- grad_v_bias: float32 [1600], P('shard')
- grad_out_weight: float32 [1600, 1600], P('shard')
- grad_out_bias: float32 [1600], P('shard')
- grad_ln2_gain: float32 [1600], P('shard')
- grad_ln2_bias: float32 [1600], P('shard')
- grad_fc_weight: float32 [1600, 6400], P('shard')
- grad_fc_bias: float32 [6400], P('shard')
- grad_proj_weight: float32 [6400, 1600], P('shard')
- grad_proj_bias: float32 [1600], P('shard')
Inputs may be any that keep to these rules, and one draw needn't show every extreme that they name: Each row's 4 lengths are positive and sum to 1024.
All inputs are finite; a program needn't handle non-finite values.
Results may differ from a plain program's by a relative error of at most 0.024.
Values may be sent and summed in bfloat16 or wider, within the bound.
No kernel may reach another device: no remote copies, remote signals or barrier semaphores. Data moves between devices by JAX's collectives and lax.ppermute only.
A program may use at most 256 MiB of HBM per device.

v0:
```python
import jax
import jax.numpy as jnp
from jax import lax
from jax.experimental import pallas as pl
from jax.experimental.pallas import tpu as pltpu
from jax.sharding import Mesh
from jax.sharding import PartitionSpec as P

HEADS = 25
HEAD_DIM = 64
EPSILON = 1e-05
LOW = jnp.bfloat16
WIDE = jnp.float32

TEAM_HEADS = 4
SPAN = TEAM_HEADS * HEAD_DIM
SHARD = 200
BLOCK = 256
CARRY = 208
WIDTH = 1600
LANES = 1664
ROWS = 128
FF_PART = 800
PIECE = 56
PIECE_STEP = 48
VMEM_LIMIT = 60 * 1024 * 1024
SMALL_LIMIT = 24 * 1024 * 1024


def after(value, *others):
    if not jax.tree.leaves(others):
        return value
    return lax.optimization_barrier((value, others))[0]


def z_swap(value, step):
    return lax.ppermute(value, "z", [(i, i ^ step) for i in range(4)])


def x_swap(value, step):
    return lax.ppermute(value, "x", [(i, i ^ step) for i in range(4)])


def y_swap(value, step):
    return lax.ppermute(value, ("yh", "yl"), [(i, i ^ step) for i in range(4)])


def c_swap(value):
    return lax.ppermute(value, "c", [(0, 1), (1, 0)])


def team_swap(value, slot):
    return lax.ppermute(value, ("c", "z"), [(i, i ^ slot) for i in range(8)])


def turn(value):
    return lax.ppermute(value, ("c", "yl"), [(0, 0), (1, 2), (2, 1), (3, 3)])


def y_swap_some(value, step, sender_diagonal):
    pairs = []
    for yh in range(2):
        for c in range(2):
            for yl in range(2):
                if (c == yl) == sender_diagonal:
                    y = (yh * 2 + yl) ^ step
                    pairs.append((yh * 4 + c * 2 + yl, (y // 2) * 4 + c * 2 + y % 2))
    return lax.ppermute(value, ("yh", "c", "yl"), pairs)


def x_swap_diagonal(value, step):
    pairs = []
    for x in range(4):
        for c in range(2):
            pairs.append((x * 4 + c * 3, (x ^ step) * 4 + c * 3))
    return lax.ppermute(value, ("x", "c", "yl"), pairs)


def pick(blocks, index):
    return lax.dynamic_index_in_dim(blocks, index, 0, keepdims=False)


DOWN = (((0,), (0,)), ((), ()))


ME, MEMBER, CORE, X, YL, Z = range(6)

def cost(microseconds):
    return pl.CostEstimate(flops=microseconds * 10**9, bytes_accessed=0, transcendentals=0)


SMEM = pl.BlockSpec(memory_space=pltpu.SMEM)
VMEM = pl.BlockSpec(memory_space=pltpu.VMEM)
ANY = pl.BlockSpec(memory_space=pltpu.HBM)


def like(shape, dtype=LOW):
    return jax.ShapeDtypeStruct(shape, dtype)


def whole_call(body, name, outs, *args, scratch=(), limit=SMALL_LIMIT):
    return pl.pallas_call(
        body,
        in_specs=[SMEM] + [VMEM] * (len(args) - 1),
        out_specs=[VMEM] * len(outs),
        out_shape=list(outs),
        scratch_shapes=list(scratch),
        compiler_params=pltpu.CompilerParams(vmem_limit_bytes=limit),
        cost_estimate=cost(0),
        name=name,
    )(*args)


def held_call(body, name, outs, at, *args, scratch=(), rows=None):
    count, made = len(args), len(outs)
    heights = [a.shape[0] if rows is None else min(rows, a.shape[0]) for a in args]

    def run(at_ref, *refs):
        sources, results, rest = refs[:count], refs[count : count + made], refs[count + made :]
        targets, others, sems = rest[:count], rest[count:-1], rest[-1]
        pairs = [(f.at[pl.ds(0, h)], t) for f, h, t in zip(sources, heights, targets)]
        for copy in load(pairs, sems):
            copy.wait()
        body(at_ref, *targets, *results, *others)

    return pl.pallas_call(
        run,
        in_specs=[SMEM] + [ANY] * count,
        out_specs=[VMEM] * made,
        out_shape=list(outs),
        scratch_shapes=[pltpu.VMEM((h,) + a.shape[1:], a.dtype) for a, h in zip(args, heights)]
        + list(scratch)
        + [pltpu.SemaphoreType.DMA((count,))],
        compiler_params=pltpu.CompilerParams(vmem_limit_bytes=VMEM_LIMIT),
        cost_estimate=cost(0),
        name=name,
    )(at, *args)


def whole_call_any(body, name, outs, args, others, scratch=()):
    return pl.pallas_call(
        body,
        in_specs=[SMEM] + [VMEM] * (len(args) - 1) + [ANY] * len(others),
        out_specs=[VMEM] * len(outs),
        out_shape=list(outs),
        scratch_shapes=list(scratch),
        compiler_params=pltpu.CompilerParams(vmem_limit_bytes=VMEM_LIMIT),
        cost_estimate=cost(0),
        name=name,
    )(*args, *others)


def block_at(index):
    return pl.ds(pl.multiple_of(index * BLOCK, BLOCK), BLOCK)


def to_blocks(source, mine, write):
    lane = lax.broadcasted_iota(jnp.int32, (source.shape[0], BLOCK), 1)
    for s in range(8):
        block = source[:, SHARD * s : SHARD * s + BLOCK]
        write(s ^ mine, jnp.where(lane < SHARD, block, jnp.zeros_like(block)))


def from_blocks(source, mine, target):
    for s in range(8):
        block = source[:, block_at(s ^ mine)]
        target[:, SHARD * s : SHARD * s + SHARD] = block[:, :SHARD].astype(target.dtype)


def prepare_qkv_kernel(at, weight, *refs):
    held, outs, vectors, sems = refs[:9], refs[9:13], refs[13:22], refs[22]
    copies = load(list(zip(held, vectors)), sems)
    for copy in copies:
        copy.wait()
    lane = lax.broadcasted_iota(jnp.int32, (SHARD, SPAN), 1)
    for d, out in enumerate(outs):
        j = at[CORE] * 4 + (at[Z] ^ d)
        valid = lane < WIDTH - SPAN * j
        none = jnp.zeros((SHARD, SPAN), LOW)
        query = weight[:, pl.ds(pl.multiple_of(SPAN * j, SPAN), SPAN)]
        out[:SHARD, :SPAN] = jnp.where(valid, query, none)
        key = weight[:, pl.ds(pl.multiple_of(WIDTH - 64 + SPAN * j, SPAN), SPAN + 128)]
        out[:SHARD, SPAN : 2 * SPAN] = jnp.where(valid, key[:, 64 : 64 + SPAN], none)

        @pl.when(j < 6)
        def _():
            start = pl.multiple_of(2 * WIDTH + SPAN * j, 128)
            out[:SHARD, 2 * SPAN :] = weight[:, pl.ds(start, SPAN)]

        @pl.when(j >= 6)
        def _():
            out[:SHARD, 2 * SPAN :] = none

        @pl.when(j == 6)
        def _():
            out[:SHARD, 2 * SPAN : 2 * SPAN + 64] = weight[:, 3 * WIDTH - 64 :]

        out[SHARD:, :] = jnp.zeros((CARRY - SHARD, 3 * SPAN), LOW)
        for i, vector in enumerate(vectors[:8]):
            out[SHARD + i : SHARD + i + 1, :SHARD] = vector[...].reshape(1, SHARD)
        for i in range(4):
            part = vectors[8][SHARD * i : SHARD * (i + 1)]
            out[SHARD + i : SHARD + i + 1, BLOCK : BLOCK + SHARD] = part.reshape(1, SHARD)


def prepare_rest_kernel(at, fc, outer, out_half, *outs):
    pad = jnp.zeros((CARRY - SHARD, FF_PART), LOW)
    for half in range(2):

        @pl.when(at[CORE] == half)
        def _():
            out_half[:SHARD, :] = outer[:, FF_PART * half : FF_PART * (half + 1)]

    out_half[SHARD:, :] = pad
    for r in range(4):
        start, shift = FF_PART * r // 128 * 128, FF_PART * r % 128
        start = pl.multiple_of(at[CORE] * (4 * FF_PART) + start, 128)
        part = fc[:, pl.ds(start, 896)][:, shift : shift + FF_PART]
        for d, out in enumerate(outs):

            @pl.when((at[Z] ^ d) == r)
            def _():
                out[:SHARD, :] = part
                out[SHARD:, :] = pad


def normalize(inputs):
    average = jnp.mean(inputs, axis=-1, keepdims=True)
    centred = inputs - average
    spread = jnp.mean(centred * centred, axis=-1, keepdims=True)
    inverse = lax.rsqrt(spread + EPSILON)
    return centred * inverse, inverse


def norm_back(d_normed, hat, inverse, gain):
    e = d_normed * gain
    return inverse * (
        e
        - jnp.mean(e, axis=-1, keepdims=True)
        - hat * jnp.mean(e * hat, axis=-1, keepdims=True)
    )


def load(pairs, sems):
    copies = [pltpu.make_async_copy(f, t, sems.at[i]) for i, (f, t) in enumerate(pairs)]
    for copy in copies:
        copy.start()
    return copies


def weight_pairs(pieces, target):
    pairs, k = [], 0
    for piece in pieces:
        for one in [piece] if len(piece.shape) == 2 else [piece.at[0], piece.at[1]]:
            pairs.append((one, target.at[k, pl.ds(0, CARRY)]))
            k += 1
    return pairs


def clear_pad(target):
    target[:, CARRY:, :] = jnp.zeros((8, BLOCK - CARRY, target.shape[2]), LOW)


def first_kernel(at, *refs):
    token_refs, weight_refs, refs = refs[:8], refs[8:12], refs[12:]
    normed, qkv, vectors, fc_bias, tokens, weight, wide, blocks, spread, *sems = refs
    step = pl.program_id(0)

    def token_copy(k):
        target = tokens.at[k ^ at[MEMBER]]
        return pltpu.make_async_copy(token_refs[k], target, sems[1].at[k])

    @pl.when(step == 0)
    def _():
        for k in range(8):
            token_copy(k).start()
        copies = load(weight_pairs(weight_refs, weight), sems[0])
        clear_pad(weight)
        spread[...] = jnp.zeros_like(spread)
        wide[:, WIDTH:] = jnp.zeros((wide.shape[0], wide.shape[1] - WIDTH), LOW)
        for copy in copies:
            copy.wait()
        for k in range(8):
            block = weight[k ^ at[ME], SHARD:CARRY, :BLOCK].astype(WIDE)
            spread[:, SHARD * k : SHARD * (k + 1)] = block[:, :SHARD]
        vectors[...] = spread[:, :WIDTH]
        rows = weight[(at[CORE] ^ at[YL]) * 4, SHARD:CARRY, BLOCK : 2 * BLOCK].astype(WIDE)
        for i in range(4):
            fc_bias[:, SHARD * i : SHARD * (i + 1)] = rows[i : i + 1, :SHARD]
        for k in range(8):
            token_copy(k).wait()

    rows = tokens[pl.ds(step * 2, 2)].reshape(2 * ROWS, WIDTH)
    hat, _ = normalize(rows.astype(WIDE))
    low = (hat * spread[0:1, :WIDTH] + spread[1:2, :WIDTH]).astype(LOW)
    normed[...] = low
    wide[:, :WIDTH] = low

    def write(k, block):
        blocks[:, block_at(k)] = block

    to_blocks(wide, at[ME], write)
    heads = pl.ds(pl.multiple_of(SPAN * at[MEMBER], SPAN), SPAN)
    total = jnp.dot(
        blocks[...], weight[...].reshape(8 * BLOCK, 3 * SPAN), preferred_element_type=WIDE
    )
    qkv[:, :SPAN] = (total[:, :SPAN] + spread[2:3, heads]).astype(LOW)
    qkv[:, SPAN : 2 * SPAN] = total[:, SPAN : 2 * SPAN].astype(LOW)
    qkv[:, 2 * SPAN :] = (total[:, 2 * SPAN :] + spread[3:4, heads]).astype(LOW)


Q_ROWS = 256


def first(at, tokens, weight):
    rows = 8 * ROWS
    still = lambda i: (0, 0)
    down = lambda i: (i, 0)
    return pl.pallas_call(
        first_kernel,
        grid=(rows // Q_ROWS,),
        in_specs=[SMEM] + [ANY] * 12,
        out_specs=[
            pl.BlockSpec((Q_ROWS, WIDTH), down),
            pl.BlockSpec((Q_ROWS, 3 * SPAN), down),
            pl.BlockSpec((8, WIDTH), still),
            pl.BlockSpec((1, FF_PART), still),
        ],
        out_shape=[
            like((rows, WIDTH)),
            like((rows, 3 * SPAN)),
            like((8, WIDTH), WIDE),
            like((1, FF_PART), WIDE),
        ],
        scratch_shapes=[
            pltpu.VMEM((8, ROWS, WIDTH), LOW),
            pltpu.VMEM((8, BLOCK, 3 * SPAN), LOW),
            pltpu.VMEM((Q_ROWS, WIDTH + 192), LOW),
            pltpu.VMEM((Q_ROWS, 8 * BLOCK), LOW),
            pltpu.VMEM((8, 8 * BLOCK), WIDE),
            pltpu.SemaphoreType.DMA((8,)),
            pltpu.SemaphoreType.DMA((8,)),
        ],
        compiler_params=pltpu.CompilerParams(vmem_limit_bytes=VMEM_LIMIT),
        cost_estimate=cost(0),
        name="first_norm_qkv",
    )(at, *tokens, *weight)


def visible(lengths, first_row, rows, keys):
    row = first_row + lax.broadcasted_iota(jnp.int32, (rows, 1), 0)
    key = lax.broadcasted_iota(jnp.int32, (1, keys), 1)
    start = jnp.zeros_like(row)
    bound = 0
    for i in range(3):
        bound = bound + lengths[0, i]
        start = jnp.where(row >= bound, bound, start)
    return (key <= row) & (key >= start)


ACROSS = (((1,), (1,)), ((), ()))


def by_block(body):
    for i in range(8 * ROWS // Q_ROWS):
        pl.when(pl.program_id(0) == i)(lambda i=i: body(i))


def slot_rows(at, chunk):
    return pl.ds(pl.multiple_of((chunk ^ at[MEMBER]) * ROWS, ROWS), ROWS)


def attend_kernel(at, lengths, q_ref, k_ref, v_ref, mixed_ref, logsum_ref):
    def block(i):
        keys = Q_ROWS * (i + 1)
        q, k, v = q_ref[...], k_ref[:keys, :], v_ref[:keys, :]
        allowed = visible(lengths, i * Q_ROWS, Q_ROWS, keys)
        lane = lax.broadcasted_iota(jnp.int32, q.shape, 1) // HEAD_DIM
        slim = lax.broadcasted_iota(jnp.int32, logsum_ref.shape, 1)
        mixed = jnp.zeros(q.shape, WIDE)
        logsums = jnp.zeros(logsum_ref.shape, WIDE)
        for head in range(TEAM_HEADS):
            own = lane == head
            q_own = jnp.where(own, q, jnp.zeros_like(q))
            scores = lax.dot_general(q_own, k, ACROSS, preferred_element_type=WIDE)
            scores = jnp.where(allowed, scores * (HEAD_DIM**-0.5), -1e30)
            top = jnp.max(scores, axis=-1, keepdims=True)
            powers = jnp.exp(scores - top)
            total = jnp.sum(powers, axis=-1, keepdims=True)
            probs = (powers * (1.0 / total)).astype(LOW)
            mixed = jnp.where(own, jnp.dot(probs, v, preferred_element_type=WIDE), mixed)
            logsums = jnp.where(slim == head, top + jnp.log(total), logsums)
        low = mixed.astype(LOW)
        for half in range(Q_ROWS // ROWS):
            rows = slot_rows(at, i * (Q_ROWS // ROWS) + half)
            mixed_ref[rows, :] = low[ROWS * half : ROWS * (half + 1)]
        logsum_ref[...] = logsums

    by_block(block)


def attend_back_kernel(
    at, lengths, q_ref, k_ref, v_ref, logsum_ref, dmix_ref, out_ref, dk_total, dv_total
):
    scale = HEAD_DIM**-0.5

    def block(i):
        keys = Q_ROWS * (i + 1)
        if i == 0:
            dk_total[...] = jnp.zeros_like(dk_total)
            dv_total[...] = jnp.zeros_like(dv_total)
        q, k, v = q_ref[...], k_ref[:keys, :], v_ref[:keys, :]
        count = Q_ROWS // ROWS
        dmix = jnp.concatenate([dmix_ref[slot_rows(at, i * count + n), :] for n in range(count)])
        allowed = visible(lengths, i * Q_ROWS, Q_ROWS, keys)
        lane = lax.broadcasted_iota(jnp.int32, q.shape, 1) // HEAD_DIM
        dq = jnp.zeros(q.shape, WIDE)
        for head in range(TEAM_HEADS):
            own = lane == head
            q_own = jnp.where(own, q, jnp.zeros_like(q))
            dmix_own = jnp.where(own, dmix, jnp.zeros_like(dmix))
            scores = lax.dot_general(q_own, k, ACROSS, preferred_element_type=WIDE) * scale
            scores = jnp.where(allowed, scores, -1e30)
            probs = jnp.exp(scores - logsum_ref[:, head : head + 1])
            d_probs = lax.dot_general(dmix_own, v, ACROSS, preferred_element_type=WIDE)
            term = jnp.sum(probs * d_probs, axis=-1, keepdims=True)
            d_scores = (probs * (d_probs - term)).astype(LOW)
            dq = jnp.where(own, jnp.dot(d_scores, k, preferred_element_type=WIDE), dq)
            dk_total[:keys, :] += lax.dot_general(
                d_scores, q_own, DOWN, preferred_element_type=WIDE
            )
            dv_total[:keys, :] += lax.dot_general(
                probs.astype(LOW), dmix_own, DOWN, preferred_element_type=WIDE
            )
        out_ref[Q_ROWS * i : Q_ROWS * (i + 1), :SPAN] = (dq * scale).astype(LOW)
        if i == 8 * ROWS // Q_ROWS - 1:
            out_ref[:, SPAN : 2 * SPAN] = (dk_total[...] * scale).astype(LOW)
            out_ref[:, 2 * SPAN :] = dv_total[...].astype(LOW)

    by_block(block)


def attend_specs(rows):
    return [
        SMEM,
        SMEM,
        pl.BlockSpec((Q_ROWS, SPAN), lambda i: (i, 0)),
        pl.BlockSpec((rows, SPAN), lambda i: (0, 1)),
        pl.BlockSpec((rows, SPAN), lambda i: (0, 2)),
    ]


def attend(places, qkv):
    rows = qkv.shape[0]
    return pl.pallas_call(
        attend_kernel,
        grid=(rows // Q_ROWS,),
        in_specs=attend_specs(rows),
        out_specs=[
            pl.BlockSpec((rows, SPAN), lambda i: (0, 0)),
            pl.BlockSpec((Q_ROWS, 128), lambda i: (i, 0)),
        ],
        out_shape=[
            jax.ShapeDtypeStruct((rows, SPAN), LOW),
            jax.ShapeDtypeStruct((rows, 128), WIDE),
        ],
        compiler_params=pltpu.CompilerParams(vmem_limit_bytes=VMEM_LIMIT),
        cost_estimate=cost(0),
        name="attend",
    )(*places, qkv, qkv, qkv)


def attend_back(places, qkv, logsum, dmix):
    rows = qkv.shape[0]
    whole = lambda i: (0, 0)
    return pl.pallas_call(
        attend_back_kernel,
        grid=(rows // Q_ROWS,),
        in_specs=attend_specs(rows)
        + [pl.BlockSpec((Q_ROWS, 128), lambda i: (i, 0)), pl.BlockSpec((rows, SPAN), whole)],
        out_specs=pl.BlockSpec((rows, 3 * SPAN), whole),
        out_shape=like((rows, 3 * SPAN)),
        scratch_shapes=[pltpu.VMEM((rows, SPAN), WIDE)] * 2,
        compiler_params=pltpu.CompilerParams(vmem_limit_bytes=VMEM_LIMIT),
        cost_estimate=cost(0),
        name="attend_back",
    )(*places, qkv, qkv, qkv, logsum, dmix)


def middle_kernel(at, tokens, vectors, *refs):
    pieces, mine_refs, other_refs, refs = refs[:4], refs[4:8], refs[8:12], refs[12:]
    middle, normed, mixed_out, mixed, blocks, wide, mine, other, *sems = refs
    copies = load(weight_pairs(mine_refs, mine), sems[0])
    copies += load(weight_pairs(other_refs, other), sems[1])
    clear_pad(mine)
    clear_pad(other)
    for d, piece in enumerate(pieces):
        mixed[:, block_at(d ^ at[MEMBER])] = piece[:, :SPAN]
        mixed[:, block_at((4 + d) ^ at[MEMBER])] = piece[:, SPAN:]

    def write_blocks(k, block):
        blocks[:, block_at(k)] = block

    to_blocks(mixed, at[ME], write_blocks)
    mixed_out[...] = mixed[:, :WIDTH]
    for copy in copies[:8]:
        copy.wait()
    flat = (8 * BLOCK, FF_PART)
    a = jnp.dot(blocks[...], mine[...].reshape(flat), preferred_element_type=WIDE)
    for copy in copies[8:]:
        copy.wait()
    b = jnp.dot(blocks[...], other[...].reshape(flat), preferred_element_type=WIDE)
    wide[:, :FF_PART] = jnp.where(at[CORE] == 0, a, b)
    wide[:, FF_PART:] = jnp.where(at[CORE] == 0, b, a)
    total = tokens[...].astype(WIDE) + wide[...] + vectors[4:5, :]
    middle[...] = total
    hat, _ = normalize(total)
    normed[...] = (hat * vectors[5:6, :] + vectors[6:7, :]).astype(LOW)


OUT_WEIGHT_SCRATCH = [
    pltpu.VMEM((8, BLOCK, FF_PART), LOW),
    pltpu.VMEM((8, BLOCK, FF_PART), LOW),
    pltpu.SemaphoreType.DMA((8,)),
    pltpu.SemaphoreType.DMA((8,)),
]


def proj_pairs(own, first_half, second_half, target):
    rows = FF_PART // 2
    return (
        [(own.at[pl.ds(0, rows)], target.at[pl.ds(0, rows)]), (own.at[pl.ds(rows, rows)], target.at[pl.ds(rows, rows)])],
        [(first_half, target.at[pl.ds(0, rows)]), (second_half, target.at[pl.ds(rows, rows)])],
    )


def load_proj(at, refs, target, sems):
    own, got = proj_pairs(*refs, target)

    @pl.when(at[CORE] == at[YL])
    def _():
        for copy in load(own, sems):
            copy.wait()

    @pl.when(at[CORE] != at[YL])
    def _():
        for copy in load(got, sems):
            copy.wait()


def halves(i):
    return jnp.minimum(i, 1), 0


def late_halves(i):
    return jnp.maximum(i - 2, 0), 0


def write_half(step, near, far, value):
    @pl.when(step < 2)
    def _():
        near[:, :WIDTH] = value
        near[:, WIDTH:] = jnp.zeros((value.shape[0], LANES - WIDTH), LOW)

    @pl.when(step >= 2)
    def _():
        far[:, :WIDTH] = value
        far[:, WIDTH:] = jnp.zeros((value.shape[0], LANES - WIDTH), LOW)


def feed_kernel(at, bias, *refs):
    cot_refs, normed_refs, fc_refs, proj_refs = refs[:8], refs[8:16], refs[16:20], refs[20:23]
    hidden, d_in, near, far, bias_sum, normed, cot, fc, proj, wide, blocks, tall, back, *sems = (
        refs[23:]
    )
    step = pl.program_id(0)

    def normed_copy(k):
        return pltpu.make_async_copy(normed_refs[k], normed.at[k], sems[0].at[k])

    def cot_copy(k):
        return pltpu.make_async_copy(cot_refs[k], cot.at[k], sems[3].at[k])

    own, got = proj_pairs(*proj_refs, proj)
    diagonal = at[CORE] == at[YL]

    def proj_copy(i):
        return pltpu.make_async_copy(got[i][0], got[i][1], sems[2].at[i])

    @pl.when(step == 0)
    def _():
        for k in range(2):
            normed_copy(k).start()
        copies = load(weight_pairs(fc_refs, fc), sems[1])
        clear_pad(fc)
        bias_sum[...] = jnp.zeros_like(bias_sum)
        wide[:, WIDTH:] = jnp.zeros((2 * ROWS, wide.shape[1] - WIDTH), LOW)
        for copy in copies:
            copy.wait()
        for k in range(2):
            cot_copy(k).start()

        @pl.when(diagonal)
        def _():
            load(own, sems[2])

        @pl.when(jnp.logical_not(diagonal))
        def _():
            load(got, sems[2])

    for k in range(8):

        @pl.when(step == k // 2)
        def _():
            normed_copy(k).wait()

        @pl.when(step + 1 == k // 2)
        def _():
            normed_copy(k).start()
            cot_copy(k).start()

    wide[:, :WIDTH] = normed[pl.ds(step * 2, 2)].reshape(2 * ROWS, WIDTH)

    def write(k, block):
        blocks[:, block_at(k)] = block

    to_blocks(wide, at[ME], write)
    weight = fc[...].reshape(8 * BLOCK, FF_PART)
    u = jnp.dot(blocks[...], weight, preferred_element_type=WIDE) + bias[...]
    for k in range(8):

        @pl.when(step == k // 2)
        def _():
            cot_copy(k).wait()

    @pl.when(step == 0)
    def _():
        proj_copy(0).wait()
        proj_copy(1).wait()

    cot_rows = cot[pl.ds(step * 2, 2)].reshape(2 * ROWS, WIDTH)
    d_hidden = lax.dot_general(cot_rows, proj[...], ACROSS, preferred_element_type=WIDE)
    factor = (2.0 / jnp.pi) ** 0.5
    square = u * u
    bent = jnp.tanh(factor * (u + 0.044715 * (square * u)))
    half = 0.5 * (1.0 + bent)
    hidden[...] = (u * half).astype(LOW)
    slope = half + (0.5 * factor) * u * (1.0 - bent * bent) * (1.0 + (3 * 0.044715) * square)
    low = (d_hidden * slope).astype(LOW)
    d_in[...] = low
    bias_sum[...] += jnp.sum(low.astype(WIDE), axis=0, keepdims=True)
    tall[...] = lax.dot_general(low, weight, ACROSS, preferred_element_type=WIDE).astype(LOW)
    from_blocks(tall, at[ME], back)
    write_half(step, near, far, back[...])


def feed(at, normed, cot, fc, proj, bias):
    rows = 8 * ROWS
    still = lambda i: (0, 0)
    down = lambda i: (i, 0)
    return pl.pallas_call(
        feed_kernel,
        grid=(rows // Q_ROWS,),
        in_specs=[SMEM, pl.BlockSpec((1, FF_PART), still)] + [ANY] * 23,
        out_specs=[
            pl.BlockSpec((Q_ROWS, FF_PART), down),
            pl.BlockSpec((Q_ROWS, FF_PART), down),
            pl.BlockSpec((Q_ROWS, LANES), halves),
            pl.BlockSpec((Q_ROWS, LANES), late_halves),
            pl.BlockSpec((1, FF_PART), still),
        ],
        out_shape=[
            like((rows, FF_PART)),
            like((rows, FF_PART)),
            like((rows // 2, LANES)),
            like((rows // 2, LANES)),
            like((1, FF_PART), WIDE),
        ],
        scratch_shapes=[
            pltpu.VMEM((8, ROWS, WIDTH), LOW),
            pltpu.VMEM((8, ROWS, WIDTH), LOW),
            pltpu.VMEM((8, BLOCK, FF_PART), LOW),
            pltpu.VMEM((FF_PART, WIDTH), LOW),
            pltpu.VMEM((Q_ROWS, WIDTH + 192), LOW),
            pltpu.VMEM((Q_ROWS, 8 * BLOCK), LOW),
            pltpu.VMEM((Q_ROWS, 8 * BLOCK), LOW),
            pltpu.VMEM((Q_ROWS, WIDTH), LOW),
            pltpu.SemaphoreType.DMA((8,)),
            pltpu.SemaphoreType.DMA((8,)),
            pltpu.SemaphoreType.DMA((2,)),
            pltpu.SemaphoreType.DMA((8,)),
        ],
        compiler_params=pltpu.CompilerParams(vmem_limit_bytes=VMEM_LIMIT),
        cost_estimate=cost(0),
        name="feed_forward_and_back",
    )(at, bias, *cot, *normed, *fc, *proj)


def final_kernel(at, hidden, *refs):
    proj_refs, (near, far, proj, sems) = refs[:3], refs[3:]
    step = pl.program_id(0)

    @pl.when(step == 0)
    def _():
        load_proj(at, proj_refs, proj, sems)

    total = jnp.dot(hidden[...], proj[...], preferred_element_type=WIDE).astype(LOW)
    write_half(step, near, far, total)


def final_part(at, hidden, proj):
    rows = hidden.shape[0]
    return pl.pallas_call(
        final_kernel,
        grid=(rows // Q_ROWS,),
        in_specs=[SMEM, pl.BlockSpec((Q_ROWS, FF_PART), lambda i: (i, 0))] + [ANY] * 3,
        out_specs=[
            pl.BlockSpec((Q_ROWS, LANES), halves),
            pl.BlockSpec((Q_ROWS, LANES), late_halves),
        ],
        out_shape=[like((rows // 2, LANES))] * 2,
        scratch_shapes=[pltpu.VMEM((FF_PART, WIDTH), LOW), pltpu.SemaphoreType.DMA((2,))],
        compiler_params=pltpu.CompilerParams(vmem_limit_bytes=VMEM_LIMIT),
        cost_estimate=cost(0),
        name="feed_forward_out",
    )(at, hidden, *proj)


def padded_rows():
    return pl.BlockSpec((ROWS, LANES), lambda i: (0, 0))


def team_total(refs):
    total = refs[0][:, :WIDTH].astype(WIDE)
    for ref in refs[1:]:
        total = total + ref[:, :WIDTH].astype(WIDE)
    return total


def row_sum(value):
    return jnp.sum(value, axis=0, keepdims=True)


def output_kernel(at, middle, vectors, near, got, one, two, three, out):
    total = middle[...] + vectors[7:8, :]
    total = total + team_total([near, got, one, two, three])
    out[...] = jnp.transpose(total).astype(LOW)


def out_grad_kernel(at, left, left_other, right, right_other, *refs):
    outs, total = refs[:4], refs[4]
    first_core = at[CORE] == 0

    def half(ref):
        value = ref[...]
        return jnp.where(first_core, value[:, :FF_PART], value[:, FF_PART:])

    total[:FF_PART, :] = lax.dot_general(
        jnp.concatenate([half(left), half(left_other)]),
        jnp.concatenate([right[...], right_other[...]]),
        DOWN,
        preferred_element_type=WIDE,
    )
    for d, out in enumerate(outs):
        start = pl.multiple_of((at[Z] ^ d) * SHARD, 8)
        out[...] = total[pl.ds(start, CARRY), :].astype(LOW)


def out_grad(at, left, left_other, right, right_other):
    return whole_call(
        out_grad_kernel,
        "out_grad",
        [like((CARRY, WIDTH))] * 4,
        at,
        left,
        left_other,
        right,
        right_other,
        scratch=[pltpu.VMEM((FF_PART + CARRY - SHARD, WIDTH), WIDE)],
        limit=VMEM_LIMIT,
    )


def out_sum_kernel(at, own, one, two, three, out, total):
    total[...] = team_total([own, one, two, three])
    for q in range(4):
        piece = total[PIECE_STEP * q : PIECE_STEP * q + PIECE, :].astype(LOW)
        out[2 * q] = piece[:, :FF_PART]
        out[2 * q + 1] = piece[:, FF_PART:]


def second_back_kernel(at, middle, cot, vectors, near, got, *refs):
    parts, mine_refs, other_refs, refs = refs[:3], refs[3:7], refs[7:11], refs[11:]
    (d_middle, d_branch, sums), pieces, refs = refs[:3], refs[3:7], refs[7:]
    wide, tall, narrow, mine, other, *sems = refs
    copies = load(weight_pairs(mine_refs, mine), sems[0])
    copies += load(weight_pairs(other_refs, other), sems[1])
    clear_pad(mine)
    clear_pad(other)
    d_second = team_total([near, got, *parts])
    hat, inverse = normalize(middle[...])
    d_cot = cot[...].astype(WIDE)
    total = d_cot + norm_back(d_second, hat, inverse, vectors[5:6, :])
    d_middle[...] = total
    low = total.astype(LOW)
    d_branch[...] = low
    sums[0:1, :] = row_sum(d_second * hat)
    sums[1:2, :] = row_sum(d_second)
    sums[2:3, :] = row_sum(low.astype(WIDE))
    sums[3:4, :] = row_sum(d_cot)
    sums[4:8, :] = jnp.zeros((4, WIDTH), WIDE)
    wide[...] = low
    left, right = wide[:, :FF_PART], wide[:, FF_PART:]
    first_core = at[CORE] == 0
    flat = (8 * BLOCK, FF_PART)
    across = (((1,), (1,)), ((), ()))
    for copy in copies[:8]:
        copy.wait()
    part = lax.dot_general(
        jnp.where(first_core, left, right),
        mine[...].reshape(flat),
        across,
        preferred_element_type=WIDE,
    )
    for copy in copies[8:]:
        copy.wait()
    tall[...] = part + lax.dot_general(
        jnp.where(first_core, right, left),
        other[...].reshape(flat),
        across,
        preferred_element_type=WIDE,
    )
    narrow[:, WIDTH:] = jnp.zeros((ROWS, 8 * SPAN - WIDTH), LOW)
    from_blocks(tall, at[ME], narrow)
    for d, piece in enumerate(pieces):
        piece[:, :SPAN] = narrow[:, block_at(d ^ at[MEMBER])]
        piece[:, SPAN:] = narrow[:, block_at((4 + d) ^ at[MEMBER])]


def second_back(at, middle, cot, vectors, near, got, parts, mine, other):
    part = pl.BlockSpec((ROWS, WIDTH), lambda i: (0, 0))
    return pl.pallas_call(
        second_back_kernel,
        grid=(1,),
        in_specs=[SMEM, part, part, pl.BlockSpec((8, WIDTH), lambda i: (0, 0))]
        + [padded_rows()] * 5
        + [ANY] * 8,
        out_specs=[VMEM] * 7,
        out_shape=[like((ROWS, WIDTH), WIDE), like((ROWS, WIDTH)), like((8, WIDTH), WIDE)]
        + [like((ROWS, 2 * SPAN))] * 4,
        scratch_shapes=[
            pltpu.VMEM((ROWS, WIDTH), LOW),
            pltpu.VMEM((ROWS, 8 * BLOCK), WIDE),
            pltpu.VMEM((ROWS, 8 * SPAN), LOW),
        ]
        + OUT_WEIGHT_SCRATCH,
        compiler_params=pltpu.CompilerParams(vmem_limit_bytes=VMEM_LIMIT),
        cost_estimate=cost(0),
        name="second_norm_and_out_back",
    )(at, middle, cot, vectors, near, got, *parts, *mine, *other)


def first_back_kernel(at, d_qkv, *refs):
    weight_refs, (near, far, sums, weight, tall, back, sems) = refs[:4], refs[4:]
    step = pl.program_id(0)

    @pl.when(step == 0)
    def _():
        copies = load(weight_pairs(weight_refs, weight), sems)
        clear_pad(weight)
        sums[...] = row_sum(d_qkv[...].astype(WIDE))
        for copy in copies:
            copy.wait()

    rows = jnp.concatenate([d_qkv[slot_rows(at, 2 * step + n), :] for n in range(2)])
    tall[...] = lax.dot_general(
        rows, weight[...].reshape(8 * BLOCK, 3 * SPAN), ACROSS, preferred_element_type=WIDE
    ).astype(LOW)
    from_blocks(tall, at[ME], back)
    write_half(step, near, far, back[...])


def first_back(at, d_qkv, weight):
    rows = d_qkv.shape[0]
    whole = lambda i: (0, 0)
    return pl.pallas_call(
        first_back_kernel,
        grid=(rows // Q_ROWS,),
        in_specs=[SMEM, pl.BlockSpec((rows, 3 * SPAN), whole)] + [ANY] * 4,
        out_specs=[
            pl.BlockSpec((Q_ROWS, LANES), halves),
            pl.BlockSpec((Q_ROWS, LANES), late_halves),
            pl.BlockSpec((1, 3 * SPAN), whole),
        ],
        out_shape=[
            like((rows // 2, LANES)),
            like((rows // 2, LANES)),
            like((1, 3 * SPAN), WIDE),
        ],
        scratch_shapes=[
            pltpu.VMEM((8, BLOCK, 3 * SPAN), LOW),
            pltpu.VMEM((Q_ROWS, 8 * BLOCK), LOW),
            pltpu.VMEM((Q_ROWS, WIDTH), LOW),
            pltpu.SemaphoreType.DMA((8,)),
        ],
        compiler_params=pltpu.CompilerParams(vmem_limit_bytes=VMEM_LIMIT),
        cost_estimate=cost(0),
        name="qkv_back",
    )(at, d_qkv, *weight)


SUMS = (PIECE, FF_PART)


def input_kernel(at, tokens, d_middle, vectors, second_sums, fc_sum, qkv_sum, *refs):
    parts, (grad, sums, held) = refs[:5], refs[5:]
    d_first = team_total(parts)
    hat, inverse = normalize(tokens[...].astype(WIDE))
    total = d_middle[...] + norm_back(d_first, hat, inverse, vectors[0:1, :])
    grad[...] = jnp.transpose(total).astype(LOW)
    held[...] = jnp.zeros(SUMS, WIDE)
    rows = [row_sum(d_first * hat), row_sum(d_first)] + [second_sums[i : i + 1, :] for i in range(4)]
    for i, row in enumerate(rows):
        held[2 * i : 2 * i + 1, :] = row[:, :FF_PART]
        held[2 * i + 1 : 2 * i + 2, :] = row[:, FF_PART:]
    held[pl.ds(16 + at[MEMBER], 1), :] = fc_sum[...]
    held[pl.ds(24 + at[MEMBER], 1), :SPAN] = qkv_sum[:, :SPAN]
    held[pl.ds(32 + at[MEMBER], 1), :SPAN] = qkv_sum[:, 2 * SPAN :]
    sums[0] = held[...].astype(LOW)


def input_back(at, tokens, d_middle, vectors, second_sums, fc_sum, qkv_sum, parts):
    still = lambda i: (0, 0)
    part = pl.BlockSpec((ROWS, WIDTH), still)
    rows = pl.BlockSpec((8, WIDTH), still)
    return pl.pallas_call(
        input_kernel,
        grid=(1,),
        in_specs=[
            SMEM,
            part,
            part,
            rows,
            rows,
            pl.BlockSpec((1, FF_PART), still),
            pl.BlockSpec((1, 3 * SPAN), still),
        ]
        + [padded_rows()] * 5,
        out_specs=[
            pl.BlockSpec((WIDTH, ROWS), still),
            pl.BlockSpec((1,) + SUMS, lambda i: (0, 0, 0)),
        ],
        out_shape=[like((WIDTH, ROWS)), like((1,) + SUMS)],
        scratch_shapes=[pltpu.VMEM(SUMS, WIDE)],
        compiler_params=pltpu.CompilerParams(vmem_limit_bytes=SMALL_LIMIT),
        cost_estimate=cost(0),
        name="first_norm_back",
    )(at, tokens, d_middle, vectors, second_sums, fc_sum, qkv_sum, *parts)


def feed_grad_kernel(at, hidden, d_in, *refs):
    cot_refs, normed_refs, (out, normed, cot, total, tall, *sems) = refs[:8], refs[8:16], refs[16:]
    pairs = [(normed_refs[k], normed.at[k]) for k in range(8)]
    first_copies = load(pairs, sems[0])
    pairs = [(cot_refs[k], cot.at[k]) for k in range(8)]
    second_copies = load(pairs, sems[1])
    for copy in first_copies:
        copy.wait()
    total[...] = lax.dot_general(
        normed[...].reshape(8 * ROWS, WIDTH), d_in[...], DOWN, preferred_element_type=WIDE
    )
    for k in range(8):
        for q in range(4):
            start = pl.multiple_of((k ^ at[ME]) * SHARD + PIECE_STEP * q, 8)
            out[16 * q + k] = total[pl.ds(start, PIECE), :].astype(LOW)
    for copy in second_copies:
        copy.wait()
    tall[...] = lax.dot_general(
        hidden[...], cot[...].reshape(8 * ROWS, WIDTH), DOWN, preferred_element_type=WIDE
    )
    for q in range(4):
        for half in range(2):
            lanes = slice(FF_PART * half, FF_PART * (half + 1))
            for k in range(4):
                start = SHARD * q + PIECE_STEP * k
                out[16 * q + 8 + 4 * half + k] = tall[start : start + PIECE, lanes].astype(LOW)


def feed_grad(at, normed, d_in, hidden, cot):
    rows = 8 * ROWS
    return pl.pallas_call(
        feed_grad_kernel,
        in_specs=[SMEM, VMEM, VMEM] + [ANY] * 16,
        out_specs=VMEM,
        out_shape=like((64, PIECE, FF_PART)),
        scratch_shapes=[
            pltpu.VMEM((8, ROWS, WIDTH), LOW),
            pltpu.VMEM((8, ROWS, WIDTH), LOW),
            pltpu.VMEM((WIDTH, FF_PART), WIDE),
            pltpu.VMEM((FF_PART, WIDTH), WIDE),
            pltpu.SemaphoreType.DMA((8,)),
            pltpu.SemaphoreType.DMA((8,)),
        ],
        compiler_params=pltpu.CompilerParams(vmem_limit_bytes=VMEM_LIMIT),
        cost_estimate=cost(0),
        name="feed_forward_grad",
    )(at, hidden, d_in, *cot, *normed)


def qkv_grad_kernel(at, normed, d_qkv, *refs):
    outs, total = refs[:4], refs[4]
    total[:, 3 * SPAN :] = jnp.zeros((WIDTH, FF_PART - 3 * SPAN), WIDE)
    total[:, : 3 * SPAN] = lax.dot_general(
        normed[...], d_qkv[...], DOWN, preferred_element_type=WIDE
    )
    for d, out in enumerate(outs):
        place = pl.multiple_of((at[X] ^ d) * PIECE_STEP, 8)
        for k in range(8):
            start = pl.multiple_of((k ^ at[ME]) * SHARD + place, 8)
            out[k] = total[pl.ds(start, PIECE), :].astype(LOW)


def added(refs, k):
    total = refs[0][k].astype(WIDE)
    for ref in refs[1:]:
        total = total + ref[k].astype(WIDE)
    return total.astype(LOW)


def feed_mid_kernel(at, total, half_got, keep, give_fc, give_proj):
    own = at[CORE] == at[YL]
    keep[:4] = total[:4]
    give_fc[...] = total[4:8]
    mine, other = total[pl.ds(8 + 4 * at[CORE], 4)], half_got[...]
    keep[4:] = jnp.where(own, mine, other)
    give_proj[...] = jnp.where(own, other, mine)


def add_halves_kernel(at, keep, first_half, second_half, out):
    count = first_half.shape[0]
    for k in range(keep.shape[0]):
        half = (first_half, k) if k < count else (second_half, k - count)
        out[k] = (keep[k].astype(WIDE) + half[0][half[1]].astype(WIDE)).astype(LOW)


def split_sum_kernel(at, one, two, *outs):
    place = 0
    for out in outs:
        for k in range(out.shape[0]):
            out[k] = added((one, two), place)
            place += 1


def qkv_x_kernel(at, *refs):
    parts, out_total, sums, (keep, give_one, give_two) = refs[:4], refs[4], refs[5], refs[6:]
    for k in range(3):
        keep[k] = added(parts, k)
        give_one[k] = added(parts, 4 + k)
    keep[3] = sums[0]
    give_one[3] = sums[0]
    keep[4] = added(parts, 3)
    give_two[0] = added(parts, 7)
    for k in range(2):
        keep[5 + k] = out_total[k]
        give_two[1 + k] = out_total[k]


def qkv_y_kernel(at, half, last, own, one, two, three, rest, sums):
    pair = (half, last)
    own[0] = added(pair, 0)
    total = added(pair, 3)
    sums[0] = total
    for out, place in ((one, 1), (two, 2), (three, 4)):
        out[0] = added(pair, place)
        out[1] = total
    for k in range(2):
        rest[k] = added(pair, 5 + k)


def qkv_z_kernel(at, own, sums, one, two, three, rest, out):
    out[0] = own[0]
    total = sums[0].astype(WIDE)
    for k, got in enumerate((one, two, three)):
        out[1 + k] = got[0]
        total = total + got[1].astype(WIDE)
    out[4:6] = rest[...]
    out[6] = total.astype(LOW)


def feed_z_kernel(at, own, one, two, three, rest, out):
    for k, got in enumerate((own, one, two, three)):
        out[k] = got[0]
    out[4:] = rest[...]


def place_feed_kernel(at, mine, other, fc, proj):
    for c in range(2):
        for q in range(4):
            count = PIECE_STEP if q < 3 else PIECE

            def block(k):
                return jnp.where(at[CORE] == c, mine[q, k], other[q, k]).astype(WIDE)

            for z in range(4):
                j = c * 4 + z
                fc[PIECE_STEP * q : PIECE_STEP * q + count, FF_PART * j : FF_PART * (j + 1)] = block(
                    z ^ at[Z]
                )[:count]
            for k in range(4):
                rows = PIECE_STEP if k < 3 else PIECE
                row = SHARD * q + PIECE_STEP * k
                proj[row : row + rows, FF_PART * c : FF_PART * (c + 1)] = block(4 + k)[:rows]


def place_qkv_kernel(at, *refs):
    mine, other, (qkv, out), refs = refs[:4], refs[4:8], refs[8:10], refs[10:]
    vectors, held, scratch = refs[:9], refs[9], refs[10:]
    for k in range(4):
        held[0, k] = mine[k][...]
        held[1, k] = other[k][...]
    own = jnp.where(at[CORE] == at[YL], 0, 1)
    for q in range(4):
        count = PIECE_STEP if q < 3 else PIECE
        rows = slice(PIECE_STEP * q, PIECE_STEP * q + count)
        for c in range(2):
            for z in range(4):
                block = held[c ^ at[CORE], q ^ at[X], z ^ at[Z]].astype(WIDE)
                for start, stop, target in qkv_columns(c * 4 + z):
                    qkv[rows, target : target + stop - start] = block[:count, start:stop]
        for half in range(2):
            block = held[own, q ^ at[X], 4 + half].astype(WIDE)
            out[rows, FF_PART * half : FF_PART * (half + 1)] = block[:count]
    total = held[0, 0, 6].astype(WIDE)
    for core in range(2):
        for k in range(4):
            if core + k:
                total = total + held[core, k, 6].astype(WIDE)
    place_vectors(at, total, *vectors, *scratch)


def place_vectors(at, total, *refs):
    outs, (small, joined) = refs[:9], refs[9:]
    small[...] = total
    for i in range(6):
        row = small[pl.ds(2 * i + at[ME] // 4, 1), :]
        for k in range(4):

            @pl.when(at[ME] % 4 == k)
            def _():
                outs[i][...] = row[:, SHARD * k : SHARD * (k + 1)].reshape(SHARD)

    outs[6][...] = small[pl.ds(16 + at[ME], 1), :].reshape(FF_PART)
    for n in range(2):
        for k in range(8):
            at_row = 24 + 8 * n + k
            joined[:, SPAN * k : SPAN * (k + 1)] = small[at_row : at_row + 1, :SPAN]
        for k in range(8):

            @pl.when(at[ME] == k)
            def _():
                outs[7 + n][...] = joined[:, SHARD * k : SHARD * (k + 1)].reshape(SHARD)


def qkv_columns(j):
    count = min(SPAN, WIDTH - SPAN * j)
    if count <= 0:
        return []
    return [(SPAN * p, SPAN * p + count, WIDTH * p + SPAN * j) for p in range(3)]


def gather_rows(block, *gates, late=()):
    beside = c_swap(block)
    sent = after(block, *gates)
    near = {d: z_swap(sent, d) for d in (1, 3, 2)}
    far = {d: c_swap(after(near[d], *late)) for d in (1, 3, 2)}
    return [block, near[1], near[2], near[3], beside, far[1], far[2], far[3]], list(near.values())


def team_parts(near, far, c_gates=(), z_gates=()):
    got = c_swap(after(far, *c_gates))
    pair = [add([v[ROWS * d : ROWS * (d + 1)] for v in (near, got)]) for d in (1, 2, 3)]
    sent = after(pair, *z_gates)
    came = [z_swap(sent[d - 1], d) for d in (1, 3, 2)]
    return [near, got] + came, sent, came


def z_blocks(own, sends, *gates):
    sends = after(sends, *gates)
    near = {d: z_swap(sends[d], d) for d in (1, 3, 2)}
    near[0] = own
    return near


def far_blocks(near, *gates):
    near = after(near, *gates)
    one, two = jnp.stack([near[0], near[1]]), jnp.stack([near[2], near[3]])
    return [one, two, y_swap(one, 1), y_swap(two, 3)]


def spread_x(value, swap):
    got = [swap(value, d) for d in (1, 3)]
    two = swap(after(value, got), 2)
    return [value, got[0], two, got[1]]


def add(values):
    total = values[0].astype(WIDE)
    for value in values[1:]:
        total = total + value.astype(WIDE)
    return total.astype(LOW)


def local(
    tokens,
    lengths,
    ln1_gain,
    ln1_bias,
    qkv_weight,
    q_bias,
    v_bias,
    out_weight,
    out_bias,
    ln2_gain,
    ln2_bias,
    fc_weight,
    fc_bias,
    proj_weight,
    proj_bias,
    cotangent,
):
    c, x, yl, z = (lax.axis_index(a) for a in ("c", "x", "yl", "z"))
    me, member = yl * 4 + z, c * 4 + z
    at = jnp.stack([me, member, c, x, yl, z]).astype(jnp.int32)

    vectors = [ln1_gain, ln1_bias, q_bias, v_bias, out_bias, ln2_gain, ln2_bias, proj_bias, fc_bias]
    own_tokens = turn(tokens)
    qkv_sends = whole_call_any(
        prepare_qkv_kernel,
        "prepare_qkv",
        [like((CARRY, 3 * SPAN))] * 4,
        [at, qkv_weight],
        vectors,
        scratch=[pltpu.VMEM(v.shape, LOW) for v in vectors] + [pltpu.SemaphoreType.DMA((9,))],
    )
    half = proj_weight.shape[0] // 2
    proj_sends = proj_weight[:half], proj_weight[half:]

    out_half, *fc_sends = whole_call(
        prepare_rest_kernel,
        "prepare_rest",
        [like((CARRY, FF_PART))] * 5,
        at,
        after(fc_weight, qkv_sends),
        out_weight,
    )
    all_tokens, tokens_came = gather_rows(own_tokens)
    qkv_near = z_blocks(qkv_sends[0], qkv_sends, own_tokens)
    other_lengths = c_swap(after(lengths, tokens_came[0]))
    places = at, jnp.where(c == yl, lengths, other_lengths)
    weight_qkv = far_blocks(qkv_near, out_half, fc_sends, places, proj_sends)
    own_cotangent = turn(after(cotangent, own_tokens))
    out_near = z_blocks(out_half, [out_half] * 4, qkv_near, all_tokens, own_cotangent)
    proj_sent = after(proj_sends, weight_qkv, out_near)
    proj_pieces = [
        proj_weight,
        y_swap_some(proj_sent[0], 1, True),
        y_swap_some(proj_sent[1], 3, True),
    ]

    normed_first, qkv, vectors_all, fc_bias_own = first(at, all_tokens, after(weight_qkv, out_near))
    all_cotangent, cotangent_came = gather_rows(own_cotangent, out_near, late=(qkv,))
    qkv = after(qkv, cotangent_came, proj_pieces)
    out_mine = far_blocks(out_near, qkv)
    fc_near = z_blocks(fc_sends[0], fc_sends, qkv)
    mixed_heads, logsum = attend(places, qkv)
    mixed_heads = after(mixed_heads, out_mine, fc_near)
    out_other = [c_swap(after(piece, mixed_heads)) for piece in out_mine]

    mixed_near = mixed_heads[: 4 * ROWS]
    mixed_got = after(c_swap(mixed_heads[4 * ROWS :]), out_other)
    mixed_sent = [
        jnp.concatenate([v[ROWS * d : ROWS * (d + 1)] for v in (mixed_near, mixed_got)], axis=1)
        for d in range(4)
    ]
    mixed_pieces = [mixed_sent[0]] + [z_swap(mixed_sent[d], d) for d in (1, 2, 3)]
    middle, normed_second, mixed = whole_call_any(
        middle_kernel,
        "out_and_second_norm",
        [like((ROWS, WIDTH), WIDE), like((ROWS, WIDTH)), like((ROWS, WIDTH))],
        [at, own_tokens, vectors_all] + mixed_pieces,
        out_mine + out_other,
        scratch=[
            pltpu.VMEM((ROWS, 8 * SPAN), LOW),
            pltpu.VMEM((ROWS, 8 * BLOCK), LOW),
            pltpu.VMEM((ROWS, WIDTH), WIDE),
        ]
        + OUT_WEIGHT_SCRATCH,
    )

    all_second, second_came = gather_rows(normed_second)
    weight_fc = far_blocks(fc_near, normed_second)
    mixed_other = c_swap(after(mixed, second_came))
    hidden, d_hidden_in, d_second_near, d_second_far, fc_bias_sum = feed(
        at, all_second, all_cotangent, weight_fc, proj_pieces, fc_bias_own
    )
    d_second_parts, d_second_sent, d_second_came = team_parts(d_second_near, d_second_far)

    hidden_late = after(hidden, d_second_sent)
    feed_pieces = feed_grad(at, all_second, d_hidden_in, hidden_late, all_cotangent)
    feed_total = lax.psum_scatter(
        after(feed_pieces, d_second_came), "x", scatter_dimension=0, tiled=True
    )

    d_middle, d_branch, second_sums, *d_mixed = second_back(
        at,
        middle,
        own_cotangent,
        after(vectors_all, feed_pieces),
        d_second_parts[0],
        d_second_parts[1],
        d_second_parts[2:],
        out_mine,
        out_other,
    )
    d_got = [d_mixed[0]] + [z_swap(d_mixed[d], d) for d in (1, 2, 3)]
    out_sent = out_grad(at, mixed, mixed_other, d_branch, c_swap(d_branch))
    d_keep = jnp.concatenate([v[:, :SPAN] for v in d_got])
    d_give = jnp.concatenate([v[:, SPAN:] for v in d_got])
    d_mixed_heads = jnp.concatenate([d_keep, c_swap(after(d_give, out_sent))])
    out_late = after(out_sent, d_give)
    out_came = [z_swap(out_late[d], d) for d in (1, 3)]
    d_qkv = attend_back(places, qkv, logsum, d_mixed_heads)
    d_qkv = after(d_qkv, out_came)
    out_came.append(z_swap(after(out_late[2], out_came), 2))

    def blocks_call(body, name, counts, *args):
        outs = [like((count, PIECE, FF_PART)) for count in counts]
        return whole_call(body, name, outs, at, *args)

    qkv_pieces = whole_call(
        qkv_grad_kernel,
        "qkv_grad",
        [like((8, PIECE, FF_PART))] * 4,
        at,
        normed_first,
        d_qkv,
        scratch=[pltpu.VMEM((WIDTH, FF_PART), WIDE)],
        limit=VMEM_LIMIT,
    )
    qkv_got = [x_swap(qkv_pieces[d], d) for d in (1, 3)]
    d_first_near, d_first_far, qkv_sums = first_back(at, after(d_qkv, qkv_pieces), weight_qkv)
    qkv_got.append(x_swap(after(qkv_pieces[2], qkv_got), 2))
    d_first_parts, d_first_sent, d_first_came = team_parts(
        d_first_near, d_first_far, (qkv_got[:2], out_came)
    )
    (out_pieces,) = held_call(
        out_sum_kernel,
        "out_sum",
        [like((8, PIECE, FF_PART))],
        at,
        out_sent[0],
        *out_came,
        scratch=[pltpu.VMEM((CARRY, WIDTH), WIDE)],
    )
    out_total = lax.psum_scatter(out_pieces, "x", scatter_dimension=0, tiled=True)
    feed_total = after(feed_total, d_first_sent)
    half_got = c_swap(lax.dynamic_slice_in_dim(feed_total, 12 - 4 * c, 4, 0))
    feed_keep, give_fc, give_proj = blocks_call(
        feed_mid_kernel, "feed_mid", [8, 4, 4], feed_total, half_got
    )
    feed_y = [y_swap(give_fc, 1), y_swap(give_proj, 3)]
    (feed_half,) = blocks_call(
        add_halves_kernel, "feed_half", [8], after(feed_keep, d_first_came), *feed_y
    )
    feed_last = y_swap(feed_half, 2)
    grad_low, sums = input_back(
        at,
        own_tokens,
        d_middle,
        after(vectors_all, feed_half),
        second_sums,
        fc_bias_sum,
        qkv_sums,
        d_first_parts,
    )
    grad_turned = turn(grad_low)
    input_grad = jnp.transpose(grad_turned.astype(WIDE))

    qkv_keep, give_one, give_two = held_call(
        qkv_x_kernel,
        "qkv_x",
        [like((count, PIECE, FF_PART)) for count in (7, 4, 3)],
        at,
        qkv_pieces[0],
        *qkv_got,
        out_total,
        sums,
    )
    qkv_y = [y_swap(give_one, 1), y_swap(give_two, 3)]
    feed_own, feed_one, feed_two, feed_three, feed_rest = blocks_call(
        split_sum_kernel, "feed_y", [1, 1, 1, 1, 4], after(feed_half, give_one), feed_last
    )
    feed_z = [z_swap(part, d) for d, part in ((1, feed_one), (2, feed_two), (3, feed_three))]
    final_near, final_far = final_part(at, after(hidden, feed_own), proj_pieces)
    (qkv_half,) = blocks_call(add_halves_kernel, "qkv_half", [7], after(qkv_keep, final_far), *qkv_y)
    qkv_last = y_swap(qkv_half, 2)
    (feed_rows,) = blocks_call(
        feed_z_kernel, "feed_z", [8], after(feed_own, qkv_half), *feed_z, feed_rest
    )
    feed_rows = lax.all_gather(feed_rows, "x", axis=0)
    final_parts, final_sent, final_came = team_parts(final_near, after(final_far, qkv_half))
    qkv_own, qkv_one, qkv_two, qkv_three, qkv_rest, sums_total = blocks_call(
        qkv_y_kernel, "qkv_y", [1, 2, 2, 2, 2, 1], after(qkv_half, final_sent, grad_turned), qkv_last
    )
    qkv_z = [z_swap(part, d) for d, part in ((1, qkv_one), (2, qkv_two), (3, qkv_three))]
    (qkv_rows,) = blocks_call(
        qkv_z_kernel, "qkv_z", [7], after(qkv_own, final_came), sums_total, *qkv_z, qkv_rest
    )
    qkv_rows = spread_x(qkv_rows, x_swap)
    (output_low,) = held_call(
        output_kernel,
        "output_rows",
        [like((WIDTH, ROWS))],
        at,
        middle,
        after(vectors_all, qkv_rows[0]),
        *final_parts,
        rows=ROWS,
    )
    output = jnp.transpose(turn(output_low))
    grad_fc, grad_proj = whole_call(
        place_feed_kernel,
        "place_feed",
        [like((SHARD, 8 * FF_PART), WIDE), like((FF_PART, WIDTH), WIDE)],
        at,
        feed_rows,
        c_swap(after(feed_rows, qkv_rows[1], qkv_rows[3])),
        limit=VMEM_LIMIT,
    )
    qkv_other = [c_swap(after(part, output, grad_fc)) for part in qkv_rows]
    vector_shapes = [like((SHARD,), WIDE)] * 6 + [like((FF_PART,), WIDE)]
    vector_shapes += [like((SHARD,), WIDE)] * 2
    grad_qkv, grad_out, *vector_grads = whole_call(
        place_qkv_kernel,
        "place_qkv",
        [like((SHARD, 3 * WIDTH), WIDE), like((SHARD, WIDTH), WIDE)] + vector_shapes,
        at,
        *qkv_rows,
        *qkv_other,
        scratch=[
            pltpu.VMEM((2, 4, 7) + SUMS, LOW),
            pltpu.VMEM(SUMS, WIDE),
            pltpu.VMEM((1, 8 * SPAN), WIDE),
        ],
        limit=VMEM_LIMIT,
    )

    g_gain_one, g_bias_one, g_gain_two, g_bias_two, g_out_b, g_proj_b = vector_grads[:6]
    g_fc_b, g_query_b, g_value_b = vector_grads[6:]

    return (
        output,
        input_grad,
        g_gain_one,
        g_bias_one,
        grad_qkv,
        g_query_b,
        g_value_b,
        grad_out,
        g_out_b,
        g_gain_two,
        g_bias_two,
        grad_fc,
        g_fc_b,
        grad_proj,
        g_proj_b,
    )


def solution(mesh):
    fine = Mesh(mesh.devices.reshape(2, 4, 2, 2, 4), ("yh", "x", "c", "yl", "z"))
    group, owner = ("yh", "x", "c"), ("yl", "z")
    everyone = group + owner
    vector, matrix = P(owner), P(owner, None)
    rows = P(everyone, None)
    return jax.shard_map(
        local,
        mesh=fine,
        in_specs=(
            rows,
            P(group, None),
            vector,
            vector,
            matrix,
            vector,
            vector,
            matrix,
            vector,
            vector,
            vector,
            matrix,
            vector,
            matrix,
            vector,
            rows,
        ),
        out_specs=(
            rows,
            rows,
            vector,
            vector,
            matrix,
            vector,
            vector,
            matrix,
            vector,
            vector,
            vector,
            matrix,
            vector,
            matrix,
            vector,
        ),
        check_vma=False,
    )
```

profile of v0, /device:TPU:27, one launch (start us, length us, event | category | flops | bytes accessed | tf_op | source)
XLA Modules:
  0.0 497.7 jit_solution(10876445993074099807)
XLA Ops:
  11.6 4.1 prepare_qkv.1
  15.8 3.4 collective-permute-start.9
  22.3 3.4 fusion
  34.1 13.6 %collective-permute-start.11 = (s32[1,4]{1,0:T(1,128)S(1)}, s32[1,4]{1,0:T(1,128)S(1)}, u32[]{:S(2)}, u32[]{:S(2)}) collective-permute-start(s32[1,4]{1,0:T(1,128)S(1)} %copy-done.92), channel_id=1, source_target_pairs={{0,8},{8,0},{1,9},{9,1},{2,10},{10,2},{3,11},{11,3},{4,12},{12,4},... | collective-permute-start | bytes 56 | tf_op jit(solution)/shard_map/ppermute | solution.py:49
  51.2 4.6 collective-permute-start.7
  64.1 10.3 %collective-permute-done.12.refs_10_.refs_2_ = bf16[2,208,768]{2,1,0:T(8,128)(2,1)S(1)} collective-permute-done((bf16[2,208,768]{2,1,0:T(8,128)(2,1)S(1)}, bf16[2,208,768]{2,1,0:T(8,128)(2,1)S(1)}, u32[]{:S(2)}, u32[]{:S(2)}) %collective-permute-start.12) | collective-permute-done | bytes 639008 | tf_op jit(solution)/shard_map/ppermute | solution.py:45
  81.9 4.6 collective-permute-start.22
  90.1 12.4 %first_norm_qkv.1 = (bf16[1024,1600]{1,0:T(8,128)(2,1)}, bf16[1024,768]{1,0:T(8,128)(2,1)}, f32[8,1600]{1,0:T(8,128)}, f32[1,800]{1,0:T(1,128)}) custom-call(s32[6]{0:T(128)} %stack.81.at.at_ref, bf16[128,1600]{1,0:T(8,128)(2,1)} %copy-done.1, bf16[128,1600]{1,0:T(8,128)(2,1)} %collective-permute-done.1.refs_1_, ...), custom_call_target="tpu_custom_call" | custom-call | tf_op jit(solution)/shard_map/first_norm_qkv/pallas_call | solution.py:319
  102.5 4.2 collective-permute-done.19.refs_3_
  114.2 2.7 collective-permute-start.26
  118.0 9.1 %attend.1 = (bf16[1024,256]{1,0:T(8,128)(2,1)}, f32[1024,128]{1,0:T(8,128)}) custom-call(s32[6]{0:T(128)} %stack.81.at.at_ref, s32[1,4]{1,0:T(1,128)} %broadcast_select_fusion.lengths, bf16[1024,768]{1,0:T(8,128)(2,1)} %get-tuple-element.192.q_ref.k_ref.v_ref, bf16[1024,768]{1,0:T(8,128)(2,1)} %get-tuple-element.192.q_ref.k_ref.v_ref, ...), custom_call_target="tpu_custom_call" | custom-call | tf_op jit(solution)/shard_map/attend/pallas_call | solution.py:455
  127.1 5.8 %collective-permute-done.26 = bf16[208,800]{1,0:T(8,128)(2,1)S(1)} collective-permute-done((bf16[208,800]{1,0:T(8,128)(2,1)S(1)}, bf16[208,800]{1,0:T(8,128)(2,1)S(1)}, u32[]{:S(2)}, u32[]{:S(2)}) %collective-permute-start.26) | collective-permute-done | bytes 332832 | tf_op jit(solution)/shard_map/ppermute | solution.py:37
  155.0 7.0 %out_and_second_norm.1 = (f32[128,1600]{1,0:T(8,128)}, bf16[128,1600]{1,0:T(8,128)(2,1)}, bf16[128,1600]{1,0:T(8,128)(2,1)}) custom-call(s32[6]{0:T(128)} %stack.81.at.at_ref, bf16[128,1600]{1,0:T(8,128)(2,1)} %copy-done.1, f32[8,1600]{1,0:T(8,128)} %get-tuple-element.282.vectors.refs_1_, bf16[128,512]{1,0:T(8,128)(2,1)} %pad_maximum_fusion.7.refs_0_, ...), custom_call_target="tpu_custom_call" | custom-call | tf_op jit(solution)/shard_map/out_and_second_norm/pallas_call | solution.py:141
  165.9 3.4 collective-permute-start.43
  172.3 9.7 %collective-permute-done.41.refs_10_ = bf16[128,1600]{1,0:T(8,128)(2,1)S(1)} collective-permute-done((bf16[128,1600]{1,0:T(8,128)(2,1)}, bf16[128,1600]{1,0:T(8,128)(2,1)S(1)}, u32[]{:S(2)}, u32[]{:S(2)}) %collective-permute-start.41) | collective-permute-done | bytes 409632 | tf_op jit(solution)/shard_map/ppermute | solution.py:37
  182.0 3.1 collective-permute-start.44
  191.4 23.9 %feed_forward_and_back.1 = (bf16[1024,800]{1,0:T(8,128)(2,1)}, bf16[1024,800]{1,0:T(8,128)(2,1)}, bf16[512,1664]{1,0:T(8,128)(2,1)}, bf16[512,1664]{1,0:T(8,128)(2,1)}, f32[1,800]{1,0:T(1,128)}) custom-call(s32[6]{0:T(128)} %stack.81.at.at_ref, f32[1,800]{1,0:T(1,128)} %get-tuple-element.210.bias, bf16[128,1600]{1,0:T(8,128)(2,1)} %collective-permute-done.14.refs_0_.cot, ...), custom_call_target="tpu_custom_call" | custom-call | tf_op jit(solution)/shard_map/feed_forward_and_back/pallas_call | solution.py:661
  217.4 3.4 collective-permute-done.49.got
  223.8 3.6 collective-permute-start.51
  227.6 15.8 %feed_forward_grad.1 = bf16[64,56,800]{2,1,0:T(8,128)(2,1)} custom-call(s32[6]{0:T(128)} %stack.81.at.at_ref, bf16[1024,800]{1,0:T(8,128)(2,1)} %get-tuple-element.267.hidden, bf16[1024,800]{1,0:T(8,128)(2,1)} %get-tuple-element.223.d_in, bf16[128,1600]{1,0:T(8,128)(2,1)} %collective-permute-done.14.refs_0_.cot, ...), custom_call_target="tpu_custom_call" | custom-call | tf_op jit(solution)/shard_map/feed_forward_grad/pallas_call | solution.py:991
  248.2 8.9 %second_norm_and_out_back.1 = (f32[128,1600]{1,0:T(8,128)}, bf16[128,1600]{1,0:T(8,128)(2,1)}, f32[8,1600]{1,0:T(8,128)}, bf16[128,512]{1,0:T(8,128)(2,1)}, bf16...) custom-call(s32[6]{0:T(128)} %stack.81.at.at_ref, ...), custom_call_target="tpu_custom_call" | custom-call | tf_op jit(solution)/shard_map/second_norm_and_out_back/pallas_call | solution.py:842
  257.1 2.8 collective-permute-start.55
  262.2 4.9 collective-permute-done.53
  268.8 4.1 out_grad.1
  279.0 15.4 %attend_back.1.d_qkv = bf16[1024,768]{1,0:T(8,128)(2,1)} custom-call(s32[6]{0:T(128)} %stack.81.at.at_ref, s32[1,4]{1,0:T(1,128)} %broadcast_select_fusion.lengths, bf16[1024,768]{1,0:T(8,128)(2,1)} %get-tuple-element.192.q_ref.k_ref.v_ref, bf16[1024,768]{1,0:T(8,128)(2,1)} %get-tuple-element.192.q_ref.k_ref.v_ref, ...), custom_call_target="tpu_custom_call" | custom-call | tf_op jit(solution)/shard_map/attend_back/pallas_call | solution.py:476
  294.5 7.6 %qkv_grad.1 = (bf16[8,56,800]{2,1,0:T(8,128)(2,1)}, bf16[8,56,800]{2,1,0:T(8,128)(2,1)}, bf16[8,56,800]{2,1,0:T(8,128)(2,1)}, bf16[8,56,800]{2,1,0:T(8,128)(2,1)}) custom-call(s32[6]{0:T(128)} %stack.81.at.at_ref, bf16[1024,1600]{1,0:T(8,128)(2,1)} %get-tuple-element.208.normed, bf16[1024,768]{1,0:T(8,128)(2,1)} %attend_back.1.d_qkv), custom_call_target="tpu_custom_call" | custom-call | tf_op jit(solution)/shard_map/qkv_grad/pallas_call | solution.py:102
  305.5 10.4 %qkv_back.1 = (bf16[512,1664]{1,0:T(8,128)(2,1)}, bf16[512,1664]{1,0:T(8,128)(2,1)}, f32[1,768]{1,0:T(1,128)}) custom-call(s32[6]{0:T(128)} %stack.81.at.at_ref, bf16[1024,768]{1,0:T(8,128)(2,1)} %attend_back.1.d_qkv, bf16[2,208,768]{2,1,0:T(8,128)(2,1)} %copy-done.30, bf16[2,208,768]{2,1,0:T(8,128)(2,1)} %copy-done.31, bf16[2,208,768]{2,1,0:T(8,128)(2,1)} %copy-done.39, ...), custom_call_target="tpu_custom_call" | custom-call | tf_op jit(solution)/shard_map/qkv_back/pallas_call | solution.py:886
  315.9 5.9 %collective-permute-done.64.refs_3_ = bf16[208,1600]{1,0:T(8,128)(2,1)S(1)} collective-permute-done((bf16[208,1600]{1,0:T(8,128)(2,1)S(1)}, bf16[208,1600]{1,0:T(8,128)(2,1)S(1)}, u32[]{:S(2)}, u32[]{:S(2)}) %collective-permute-start.64) | collective-permute-done | bytes 665632 | tf_op jit(solution)/shard_map/ppermute | solution.py:37
  321.8 4.3 collective-permute-done.61.refs_1_
  328.6 4.1 out_sum.1
  342.7 3.8 collective-permute-done.67.refs_2_
  348.5 7.7 %collective-permute-done.68.refs_3_ = bf16[128,1664]{1,0:T(8,128)(2,1)S(1)} collective-permute-done((bf16[128,1664]{1,0:T(8,128)(2,1)}, bf16[128,1664]{1,0:T(8,128)(2,1)S(1)}, u32[]{:S(2)}, u32[]{:S(2)}) %collective-permute-start.68) | collective-permute-done | bytes 426016 | tf_op jit(solution)/shard_map/ppermute | solution.py:37
  363.8 4.8 collective-permute-done.63.refs_3_
  368.5 4.1 qkv_x.1
  374.1 5.4 %collective-permute-done.72.two = bf16[8,56,800]{2,1,0:T(8,128)(2,1)} collective-permute-done((bf16[8,56,800]{2,1,0:T(8,128)(2,1)}, bf16[8,56,800]{2,1,0:T(8,128)(2,1)}, u32[]{:S(2)}, u32[]{:S(2)}) %collective-permute-start.72) | collective-permute-done | bytes 716832 | tf_op jit(solution)/shard_map/ppermute | solution.py:45
  385.3 9.0 %feed_forward_out.1 = (bf16[512,1664]{1,0:T(8,128)(2,1)}, bf16[512,1664]{1,0:T(8,128)(2,1)}) custom-call(s32[6]{0:T(128)} %stack.81.at.at_ref, bf16[1024,800]{1,0:T(8,128)(2,1)} %get-tuple-element.267.hidden, bf16[800,1600]{1,0:T(8,128)(2,1)} %refs_0_.3, bf16[400,1600]{1,0:T(8,128)(2,1)} %copy-done.32, bf16[400,1600]{1,0:T(8,128)(2,1)} %collective-permute-done.22.refs_22_.refs_2_), custom_call_target="tpu_custom_call" | custom-call | tf_op jit(solution)/shard_map/feed_forward_out/pallas_call | solution.py:713
  396.6 5.0 collective-permute-start.75
  412.1 8.3 %collective-permute-done.77.last = bf16[7,56,800]{2,1,0:T(8,128)(2,1)S(1)} collective-permute-done((bf16[7,56,800]{2,1,0:T(8,128)(2,1)S(1)}, bf16[7,56,800]{2,1,0:T(8,128)(2,1)S(1)}, u32[]{:S(2)}, u32[]{:S(2)}) %collective-permute-start.77) | collective-permute-done | bytes 627232 | tf_op jit(solution)/shard_map/ppermute | solution.py:45
  421.2 3.1 collective-permute-start.82
  425.0 4.1 collective-permute-done.80.refs_6_
  429.2 2.8 collective-permute-done.81.one
  431.9 5.9 %collective-permute-done.82.two = bf16[2,56,800]{2,1,0:T(8,128)(2,1)S(1)} collective-permute-done((bf16[2,56,800]{2,1,0:T(8,128)(2,1)S(1)}, bf16[2,56,800]{2,1,0:T(8,128)(2,1)S(1)}, u32[]{:S(2)}, u32[]{:S(2)}) %collective-permute-start.82) | collective-permute-done | bytes 179232 | tf_op jit(solution)/shard_map/ppermute | solution.py:37
  440.9 12.9 %collective-permute-done.85.refs_1_ = bf16[7,56,800]{2,1,0:T(8,128)(2,1)S(1)} collective-permute-done((bf16[7,56,800]{2,1,0:T(8,128)(2,1)S(1)}, bf16[7,56,800]{2,1,0:T(8,128)(2,1)S(1)}, u32[]{:S(2)}, u32[]{:S(2)}) %collective-permute-start.85) | collective-permute-done | bytes 627232 | tf_op jit(solution)/shard_map/ppermute | solution.py:41
  455.0 3.3 collective-permute-start.91
  460.9 3.7 output_rows.1
  466.4 8.1 %place_feed.1 = (f32[200,6400]{1,0:T(8,128)}, f32[800,1600]{1,0:T(8,128)}) custom-call(s32[6]{0:T(128)} %stack.81.at.at_ref, bf16[4,8,56,800]{3,2,1,0:T(8,128)(2,1)} %bitcast.25, bf16[4,8,56,800]{3,2,1,0:T(8,128)(2,1)} %collective-permute-done.91.other), custom_call_target="tpu_custom_call" | custom-call | tf_op jit(solution)/shard_map/place_feed/pallas_call | solution.py:102
  475.3 2.7 collective-permute-start.92
  483.7 6.4 %place_qkv.1 = (f32[200,4800]{1,0:T(8,128)}, f32[200,1600]{1,0:T(8,128)}, f32[200]{0:T(256)}, f32[200]{0:T(256)}, f32[200]{0:T(256)}, /*index=5*/f32[200]{0:T(25...) custom-call(s32[6]{0:T(128)} %stack.81.at.at_ref, ...), custom_call_target="tpu_custom_call" | custom-call | tf_op jit(solution)/shard_map/place_qkv/pallas_call | solution.py:102
  (399 shorter events, 165.2 us)
Async XLA Ops:
  7.2 326.8 %reduce-scatter.5.cloned.1.call-start = ((), (), s32[]{:S(2)}) async-start(), calls=%async_computation.3 | async-start | bytes 8028160 | tf_op jit(solution)/shard_map/reduce_scatter | solution.py:1310
  15.7 16.8 %collective-permute-start.8 = (bf16[208,768]{1,0:T(8,128)(2,1)}, bf16[208,768]{1,0:T(8,128)(2,1)}, u32[]{:S(2)}, u32[]{:S(2)}) collective-permute-start(bf16[208,768]{1,0:T(8,128)(2,1)} %get-tuple-element.165), channel_id=1, source_target_pairs={{0,1},{1,0},{2,3},{3,2},{4,5},{5,4},{6,7},{7,6},{8,9},{9,8},{10,11... | collective-permute-start | bytes 958472 | tf_op jit(solution)/shard_map/ppermute | solution.py:37
  15.8 18.3 %collective-permute-start.9 = (bf16[208,768]{1,0:T(8,128)(2,1)}, bf16[208,768]{1,0:T(8,128)(2,1)}, u32[]{:S(2)}, u32[]{:S(2)}) collective-permute-start(bf16[208,768]{1,0:T(8,128)(2,1)} %get-tuple-element.166), channel_id=1, source_target_pairs={{0,2},{1,3},{2,0},{3,1},{4,6},{5,7},{6,4},{7,5},{8,10},{9,11},{10,... | collective-permute-start | bytes 958472 | tf_op jit(solution)/shard_map/ppermute | solution.py:37
  19.2 30.1 %collective-permute-start.10 = (bf16[208,768]{1,0:T(8,128)(2,1)}, bf16[208,768]{1,0:T(8,128)(2,1)}, u32[]{:S(2)}, u32[]{:S(2)}) collective-permute-start(bf16[208,768]{1,0:T(8,128)(2,1)} %get-tuple-element.167), channel_id=1, source_target_pairs={{0,3},{1,2},{2,1},{3,0},{4,7},{5,6},{6,5},{7,4},{8,11},{9,10},{10,... | collective-permute-start | bytes 958472 | tf_op jit(solution)/shard_map/ppermute | solution.py:37
  19.6 31.6 %collective-permute-start.2 = (bf16[128,1600]{1,0:T(8,128)(2,1)S(1)}, bf16[128,1600]{1,0:T(8,128)(2,1)}, u32[]{:S(2)}, u32[]{:S(2)}) collective-permute-start(bf16[128,1600]{1,0:T(8,128)(2,1)S(1)} %collective-permute-done.refs_0_.tokens), channel_id=1, source_target_pairs={{0,2},{1,3},{2,0},{3,1},{4,6},{5,7},{6,4},{7,5},{8,10},{9,11},{10,... | collective-permute-start | bytes 1228808 | tf_op jit(solution)/shard_map/ppermute | solution.py:37
  21.7 29.5 %collective-permute-start.3 = (bf16[128,1600]{1,0:T(8,128)(2,1)S(1)}, bf16[128,1600]{1,0:T(8,128)(2,1)}, u32[]{:S(2)}, u32[]{:S(2)}) collective-permute-start(bf16[128,1600]{1,0:T(8,128)(2,1)S(1)} %collective-permute-done.refs_0_.tokens), channel_id=1, source_target_pairs={{0,3},{1,2},{2,1},{3,0},{4,7},{5,6},{6,5},{7,4},{8,11},{9,10},{10,... | collective-permute-start | bytes 1228808 | tf_op jit(solution)/shard_map/ppermute | solution.py:37
  32.5 27.6 %collective-permute-start.14 = (bf16[128,1600]{1,0:T(8,128)(2,1)S(1)}, bf16[128,1600]{1,0:T(8,128)(2,1)}, u32[]{:S(2)}, u32[]{:S(2)}) collective-permute-start(bf16[128,1600]{1,0:T(8,128)(2,1)S(1)} %copy.34), channel_id=1, source_target_pairs={{0,0},{4,8},{8,4},{12,12},{1,1},{5,9},{9,5},{13,13},{2,2},{6,10},{... | collective-permute-start | bytes 1228808 | tf_op jit(solution)/shard_map/ppermute | solution.py:57
  60.3 17.6 %collective-permute-start.16 = (bf16[208,800]{1,0:T(8,128)(2,1)S(1)}, bf16[208,800]{1,0:T(8,128)(2,1)S(1)}, u32[]{:S(2)}, u32[]{:S(2)}) collective-permute-start(bf16[208,800]{1,0:T(8,128)(2,1)S(1)} %copy-done.15), channel_id=1, source_target_pairs={{0,2},{1,3},{2,0},{3,1},{4,6},{5,7},{6,4},{7,5},{8,10},{9,11},{10,... | collective-permute-start | bytes 998408 | tf_op jit(solution)/shard_map/ppermute | solution.py:37
  61.9 18.0 %collective-permute-start.17 = (bf16[208,800]{1,0:T(8,128)(2,1)S(1)}, bf16[208,800]{1,0:T(8,128)(2,1)S(1)}, u32[]{:S(2)}, u32[]{:S(2)}) collective-permute-start(bf16[208,800]{1,0:T(8,128)(2,1)S(1)} %copy-done.15), channel_id=1, source_target_pairs={{0,3},{1,2},{2,1},{3,0},{4,7},{5,6},{6,5},{7,4},{8,11},{9,10},{10,... | collective-permute-start | bytes 998408 | tf_op jit(solution)/shard_map/ppermute | solution.py:37
  79.9 28.4 %collective-permute-start.21 = (bf16[400,1600]{1,0:T(8,128)(2,1)}, bf16[400,1600]{1,0:T(8,128)(2,1)S(1)}, u32[]{:S(2)}, u32[]{:S(2)}) collective-permute-start(bf16[400,1600]{1,0:T(8,128)(2,1)} %get-tuple-element.190), channel_id=1, source_target_pairs={{0,4},{12,8},{64,68},{76,72},{1,5},{13,9},{65,69},{77,73},{2,6},{1... | collective-permute-start | bytes 3840008 | tf_op jit(solution)/shard_map/ppermute | solution.py:68
  81.9 26.3 %collective-permute-start.22 = (bf16[400,1600]{1,0:T(8,128)(2,1)}, bf16[400,1600]{1,0:T(8,128)(2,1)}, u32[]{:S(2)}, u32[]{:S(2)}) collective-permute-start(bf16[400,1600]{1,0:T(8,128)(2,1)} %get-tuple-element.191), channel_id=1, source_target_pairs={{0,68},{12,72},{64,4},{76,8},{1,69},{13,73},{65,5},{77,9},{2,70},{... | collective-permute-start | bytes 3840008 | tf_op jit(solution)/shard_map/ppermute | solution.py:68
  86.6 20.2 %collective-permute-start.19 = (bf16[128,1600]{1,0:T(8,128)(2,1)}, bf16[128,1600]{1,0:T(8,128)(2,1)}, u32[]{:S(2)}, u32[]{:S(2)}) collective-permute-start(bf16[128,1600]{1,0:T(8,128)(2,1)} %collective-permute-done.14.refs_0_.cot), channel_id=1, source_target_pairs={{0,3},{1,2},{2,1},{3,0},{4,7},{5,6},{6,5},{7,4},{8,11},{9,10},{10,... | collective-permute-start | bytes 1228808 | tf_op jit(solution)/shard_map/ppermute | solution.py:37
  88.9 19.4 %collective-permute-start.20 = (bf16[128,1600]{1,0:T(8,128)(2,1)}, bf16[128,1600]{1,0:T(8,128)(2,1)}, u32[]{:S(2)}, u32[]{:S(2)}) collective-permute-start(bf16[128,1600]{1,0:T(8,128)(2,1)} %collective-permute-done.14.refs_0_.cot), channel_id=1, source_target_pairs={{0,2},{1,3},{2,0},{3,1},{4,6},{5,7},{6,4},{7,5},{8,10},{9,11},{10,... | collective-permute-start | bytes 1228808 | tf_op jit(solution)/shard_map/ppermute | solution.py:37
  110.5 24.6 %collective-permute-start.23 = (bf16[2,208,800]{2,1,0:T(8,128)(2,1)S(1)}, bf16[2,208,800]{2,1,0:T(8,128)(2,1)}, u32[]{:S(2)}, u32[]{:S(2)}) collective-permute-start(bf16[2,208,800]{2,1,0:T(8,128)(2,1)S(1)} %pad_maximum_fusion.refs_4_.refs_3_), channel_id=1, source_target_pairs={{0,4},{4,0},{64,68},{68,64},{1,5},{5,1},{65,69},{69,65},{2,6},{6,2... | collective-permute-start | bytes 1996808 | tf_op jit(solution)/shard_map/ppermute | solution.py:45
  111.9 23.3 %collective-permute-start.24 = (bf16[2,208,800]{2,1,0:T(8,128)(2,1)S(1)}, bf16[2,208,800]{2,1,0:T(8,128)(2,1)}, u32[]{:S(2)}, u32[]{:S(2)}) collective-permute-start(bf16[2,208,800]{2,1,0:T(8,128)(2,1)S(1)} %pad_maximum_fusion.1.refs_5_.refs_4_), channel_id=1, source_target_pairs={{0,68},{4,64},{64,4},{68,0},{1,69},{5,65},{65,5},{69,1},{2,70},{6,... | collective-permute-start | bytes 1996808 | tf_op jit(solution)/shard_map/ppermute | solution.py:45
  114.2 18.8 %collective-permute-start.26 = (bf16[208,800]{1,0:T(8,128)(2,1)S(1)}, bf16[208,800]{1,0:T(8,128)(2,1)S(1)}, u32[]{:S(2)}, u32[]{:S(2)}) collective-permute-start(bf16[208,800]{1,0:T(8,128)(2,1)S(1)} %copy-done.25), channel_id=1, source_target_pairs={{0,2},{1,3},{2,0},{3,1},{4,6},{5,7},{6,4},{7,5},{8,10},{9,11},{10,... | collective-permute-start | bytes 998408 | tf_op jit(solution)/shard_map/ppermute | solution.py:37
  116.9 18.2 %collective-permute-start.27 = (bf16[208,800]{1,0:T(8,128)(2,1)S(1)}, bf16[208,800]{1,0:T(8,128)(2,1)}, u32[]{:S(2)}, u32[]{:S(2)}) collective-permute-start(bf16[208,800]{1,0:T(8,128)(2,1)S(1)} %copy-done.23), channel_id=1, source_target_pairs={{0,3},{1,2},{2,1},{3,0},{4,7},{5,6},{6,5},{7,4},{8,11},{9,10},{10,... | collective-permute-start | bytes 998408 | tf_op jit(solution)/shard_map/ppermute | solution.py:37
  142.1 20.1 %collective-permute-start.36 = (bf16[128,1600]{1,0:T(8,128)(2,1)}, bf16[128,1600]{1,0:T(8,128)(2,1)S(1)}, u32[]{:S(2)}, u32[]{:S(2)}) collective-permute-start(bf16[128,1600]{1,0:T(8,128)(2,1)} %collective-permute-done.14.refs_0_.cot), channel_id=1, source_target_pairs={{0,8},{8,0},{1,9},{9,1},{2,10},{10,2},{3,11},{11,3},{4,12},{12,4},... | collective-permute-start | bytes 1228808 | tf_op jit(solution)/shard_map/ppermute | solution.py:49
  142.5 22.3 %collective-permute-start.37 = (bf16[128,1600]{1,0:T(8,128)(2,1)}, bf16[128,1600]{1,0:T(8,128)(2,1)S(1)}, u32[]{:S(2)}, u32[]{:S(2)}) collective-permute-start(bf16[128,1600]{1,0:T(8,128)(2,1)} %collective-permute-done.18.refs_1_), channel_id=1, source_target_pairs={{0,8},{8,0},{1,9},{9,1},{2,10},{10,2},{3,11},{11,3},{4,12},{12,4},... | collective-permute-start | bytes 1228808 | tf_op jit(solution)/shard_map/ppermute | solution.py:49
  143.7 22.3 %collective-permute-start.38 = (bf16[128,1600]{1,0:T(8,128)(2,1)}, bf16[128,1600]{1,0:T(8,128)(2,1)S(1)}, u32[]{:S(2)}, u32[]{:S(2)}) collective-permute-start(bf16[128,1600]{1,0:T(8,128)(2,1)} %collective-permute-done.20.refs_2_), channel_id=1, source_target_pairs={{0,8},{8,0},{1,9},{9,1},{2,10},{10,2},{3,11},{11,3},{4,12},{12,4},... | collective-permute-start | bytes 1228808 | tf_op jit(solution)/shard_map/ppermute | solution.py:49
  152.5 18.3 %collective-permute-start.39 = (bf16[128,1600]{1,0:T(8,128)(2,1)}, bf16[128,1600]{1,0:T(8,128)(2,1)S(1)}, u32[]{:S(2)}, u32[]{:S(2)}) collective-permute-start(bf16[128,1600]{1,0:T(8,128)(2,1)} %collective-permute-done.19.refs_3_), channel_id=1, source_target_pairs={{0,8},{8,0},{1,9},{9,1},{2,10},{10,2},{3,11},{11,3},{4,12},{12,4},... | collective-permute-start | bytes 1228808 | tf_op jit(solution)/shard_map/ppermute | solution.py:49
  162.3 19.7 %collective-permute-start.41 = (bf16[128,1600]{1,0:T(8,128)(2,1)}, bf16[128,1600]{1,0:T(8,128)(2,1)S(1)}, u32[]{:S(2)}, u32[]{:S(2)}) collective-permute-start(bf16[128,1600]{1,0:T(8,128)(2,1)} %get-tuple-element.214.refs_8_), channel_id=1, source_target_pairs={{0,2},{1,3},{2,0},{3,1},{4,6},{5,7},{6,4},{7,5},{8,10},{9,11},{10,... | collective-permute-start | bytes 1228808 | tf_op jit(solution)/shard_map/ppermute | solution.py:37
  164.8 20.2 %collective-permute-start.42 = (bf16[128,1600]{1,0:T(8,128)(2,1)}, bf16[128,1600]{1,0:T(8,128)(2,1)S(1)}, u32[]{:S(2)}, u32[]{:S(2)}) collective-permute-start(bf16[128,1600]{1,0:T(8,128)(2,1)} %get-tuple-element.214.refs_8_), channel_id=1, source_target_pairs={{0,3},{1,2},{2,1},{3,0},{4,7},{5,6},{6,5},{7,4},{8,11},{9,10},{10,... | collective-permute-start | bytes 1228808 | tf_op jit(solution)/shard_map/ppermute | solution.py:37
  165.9 21.7 %collective-permute-start.43 = (bf16[128,1600]{1,0:T(8,128)(2,1)}, bf16[128,1600]{1,0:T(8,128)(2,1)S(1)}, u32[]{:S(2)}, u32[]{:S(2)}) collective-permute-start(bf16[128,1600]{1,0:T(8,128)(2,1)} %get-tuple-element.214.refs_8_), channel_id=1, source_target_pairs={{0,8},{8,0},{1,9},{9,1},{2,10},{10,2},{3,11},{11,3},{4,12},{12,4},... | collective-permute-start | bytes 1228808 | tf_op jit(solution)/shard_map/ppermute | solution.py:49
  170.8 18.4 %collective-permute-start.47 = (bf16[2,208,800]{2,1,0:T(8,128)(2,1)S(1)}, bf16[2,208,800]{2,1,0:T(8,128)(2,1)S(1)}, u32[]{:S(2)}, u32[]{:S(2)}) collective-permute-start(bf16[2,208,800]{2,1,0:T(8,128)(2,1)S(1)} %pad_maximum_fusion.2.refs_16_), channel_id=1, source_target_pairs={{0,4},{4,0},{64,68},{68,64},{1,5},{5,1},{65,69},{69,65},{2,6},{6,2... | collective-permute-start | bytes 1996808 | tf_op jit(solution)/shard_map/ppermute | solution.py:45
  171.1 18.1 %collective-permute-start.48 = (bf16[2,208,800]{2,1,0:T(8,128)(2,1)S(1)}, bf16[2,208,800]{2,1,0:T(8,128)(2,1)S(1)}, u32[]{:S(2)}, u32[]{:S(2)}) collective-permute-start(bf16[2,208,800]{2,1,0:T(8,128)(2,1)S(1)} %pad_maximum_fusion.3.refs_17_), channel_id=1, source_target_pairs={{0,68},{4,64},{64,4},{68,0},{1,69},{5,65},{65,5},{69,1},{2,70},{6,... | collective-permute-start | bytes 1996808 | tf_op jit(solution)/shard_map/ppermute | solution.py:45
  223.0 20.4 %collective-permute-start.50 = (bf16[128,1664]{1,0:T(8,128)(2,1)S(1)}, bf16[128,1664]{1,0:T(8,128)(2,1)S(1)}, u32[]{:S(2)}, u32[]{:S(2)}) collective-permute-start(bf16[128,1664]{1,0:T(8,128)(2,1)S(1)} %get-tuple-element.315), channel_id=1, source_target_pairs={{0,1},{1,0},{2,3},{3,2},{4,5},{5,4},{6,7},{7,6},{8,9},{9,8},{10,11... | collective-permute-start | bytes 1277960 | tf_op jit(solution)/shard_map/ppermute | solution.py:37
  223.8 21.3 %collective-permute-start.51 = (bf16[128,1664]{1,0:T(8,128)(2,1)S(1)}, bf16[128,1664]{1,0:T(8,128)(2,1)S(1)}, u32[]{:S(2)}, u32[]{:S(2)}) collective-permute-start(bf16[128,1664]{1,0:T(8,128)(2,1)S(1)} %get-tuple-element.313), channel_id=1, source_target_pairs={{0,3},{1,2},{2,1},{3,0},{4,7},{5,6},{6,5},{7,4},{8,11},{9,10},{10,... | collective-permute-start | bytes 1277960 | tf_op jit(solution)/shard_map/ppermute | solution.py:37
  227.4 18.8 %collective-permute-start.52 = (bf16[128,1664]{1,0:T(8,128)(2,1)S(1)}, bf16[128,1664]{1,0:T(8,128)(2,1)S(1)}, u32[]{:S(2)}, u32[]{:S(2)}) collective-permute-start(bf16[128,1664]{1,0:T(8,128)(2,1)S(1)} %get-tuple-element.314), channel_id=1, source_target_pairs={{0,2},{1,3},{2,0},{3,1},{4,6},{5,7},{6,4},{7,5},{8,10},{9,11},{10,... | collective-permute-start | bytes 1277960 | tf_op jit(solution)/shard_map/ppermute | solution.py:37
  247.0 121.5 %reduce-scatter.3.cloned.1.call-start = ((), (), s32[]{:S(2)}) async-start(), calls=%async_computation.2 | async-start | bytes 1003520 | tf_op jit(solution)/shard_map/reduce_scatter | solution.py:1365
  247.0 20.3 %collective-permute-start.56 = (bf16[128,1600]{1,0:T(8,128)(2,1)S(1)}, bf16[128,1600]{1,0:T(8,128)(2,1)S(1)}, u32[]{:S(2)}, u32[]{:S(2)}) collective-permute-start(bf16[128,1600]{1,0:T(8,128)(2,1)S(1)} %copy-done.70), channel_id=1, source_target_pairs={{0,8},{8,0},{1,9},{9,1},{2,10},{10,2},{3,11},{11,3},{4,12},{12,4},... | collective-permute-start | bytes 1228808 | tf_op jit(solution)/shard_map/ppermute | solution.py:49
  272.9 21.5 %collective-permute-start.59 = (bf16[208,1600]{1,0:T(8,128)(2,1)}, bf16[208,1600]{1,0:T(8,128)(2,1)S(1)}, u32[]{:S(2)}, u32[]{:S(2)}) collective-permute-start(bf16[208,1600]{1,0:T(8,128)(2,1)} %get-tuple-element.237), channel_id=1, source_target_pairs={{0,1},{1,0},{2,3},{3,2},{4,5},{5,4},{6,7},{7,6},{8,9},{9,8},{10,11... | collective-permute-start | bytes 1996808 | tf_op jit(solution)/shard_map/ppermute | solution.py:37
  273.9 20.5 %collective-permute-start.60 = (bf16[208,1600]{1,0:T(8,128)(2,1)}, bf16[208,1600]{1,0:T(8,128)(2,1)S(1)}, u32[]{:S(2)}, u32[]{:S(2)}) collective-permute-start(bf16[208,1600]{1,0:T(8,128)(2,1)} %get-tuple-element.238), channel_id=1, source_target_pairs={{0,3},{1,2},{2,1},{3,0},{4,7},{5,6},{6,5},{7,4},{8,11},{9,10},{10,... | collective-permute-start | bytes 1996808 | tf_op jit(solution)/shard_map/ppermute | solution.py:37
  302.0 24.0 %collective-permute-start.61 = (bf16[8,56,800]{2,1,0:T(8,128)(2,1)}, bf16[8,56,800]{2,1,0:T(8,128)(2,1)S(1)}, u32[]{:S(2)}, u32[]{:S(2)}) collective-permute-start(bf16[8,56,800]{2,1,0:T(8,128)(2,1)} %get-tuple-element.241), channel_id=1, source_target_pairs={{0,16},{16,0},{32,48},{48,32},{1,17},{17,1},{33,49},{49,33},{2,18}... | collective-permute-start | bytes 2150408 | tf_op jit(solution)/shard_map/ppermute | solution.py:41
  302.5 24.5 %collective-permute-start.62 = (bf16[8,56,800]{2,1,0:T(8,128)(2,1)}, bf16[8,56,800]{2,1,0:T(8,128)(2,1)S(1)}, u32[]{:S(2)}, u32[]{:S(2)}) collective-permute-start(bf16[8,56,800]{2,1,0:T(8,128)(2,1)} %get-tuple-element.242), channel_id=1, source_target_pairs={{0,48},{16,32},{32,16},{48,0},{1,49},{17,33},{33,17},{49,1},{2,50}... | collective-permute-start | bytes 2150408 | tf_op jit(solution)/shard_map/ppermute | solution.py:41
  304.3 17.6 %collective-permute-start.64 = (bf16[208,1600]{1,0:T(8,128)(2,1)S(1)}, bf16[208,1600]{1,0:T(8,128)(2,1)S(1)}, u32[]{:S(2)}, u32[]{:S(2)}) collective-permute-start(bf16[208,1600]{1,0:T(8,128)(2,1)S(1)} %copy-done.94), channel_id=1, source_target_pairs={{0,2},{1,3},{2,0},{3,1},{4,6},{5,7},{6,4},{7,5},{8,10},{9,11},{10,... | collective-permute-start | bytes 1996808 | tf_op jit(solution)/shard_map/ppermute | solution.py:37
  332.7 122.3 %all-gather.3.cloned.1.call-start = ((), (), s32[]{:S(2)}) async-start(), calls=%async_computation.4 | async-start | bytes 4014080 | tf_op jit(solution)/shard_map/all_gather | solution.py:1410
  336.5 19.6 %collective-permute-start.68 = (bf16[128,1664]{1,0:T(8,128)(2,1)}, bf16[128,1664]{1,0:T(8,128)(2,1)S(1)}, u32[]{:S(2)}, u32[]{:S(2)}) collective-permute-start(bf16[128,1664]{1,0:T(8,128)(2,1)} %get-tuple-element.310), channel_id=1, source_target_pairs={{0,3},{1,2},{2,1},{3,0},{4,7},{5,6},{6,5},{7,4},{8,11},{9,10},{10,... | collective-permute-start | bytes 1277960 | tf_op jit(solution)/shard_map/ppermute | solution.py:37
  338.4 19.6 %collective-permute-start.69 = (bf16[128,1664]{1,0:T(8,128)(2,1)}, bf16[128,1664]{1,0:T(8,128)(2,1)S(1)}, u32[]{:S(2)}, u32[]{:S(2)}) collective-permute-start(bf16[128,1664]{1,0:T(8,128)(2,1)} %get-tuple-element.311), channel_id=1, source_target_pairs={{0,2},{1,3},{2,0},{3,1},{4,6},{5,7},{6,4},{7,5},{8,10},{9,11},{10,... | collective-permute-start | bytes 1277960 | tf_op jit(solution)/shard_map/ppermute | solution.py:37
  346.5 22.0 %collective-permute-start.63 = (bf16[8,56,800]{2,1,0:T(8,128)(2,1)S(1)}, bf16[8,56,800]{2,1,0:T(8,128)(2,1)}, u32[]{:S(2)}, u32[]{:S(2)}) collective-permute-start(bf16[8,56,800]{2,1,0:T(8,128)(2,1)S(1)} %copy-done.93), channel_id=1, source_target_pairs={{0,32},{16,48},{32,0},{48,16},{1,33},{17,49},{33,1},{49,17},{2,34}... | collective-permute-start | bytes 2150408 | tf_op jit(solution)/shard_map/ppermute | solution.py:41
  359.6 19.9 %collective-permute-start.72 = (bf16[8,56,800]{2,1,0:T(8,128)(2,1)}, bf16[8,56,800]{2,1,0:T(8,128)(2,1)}, u32[]{:S(2)}, u32[]{:S(2)}) collective-permute-start(bf16[8,56,800]{2,1,0:T(8,128)(2,1)} %feed_half.1.one), channel_id=1, source_target_pairs={{0,64},{4,68},{64,0},{68,4},{1,65},{5,69},{65,1},{69,5},{2,66},{6,... | collective-permute-start | bytes 2150408 | tf_op jit(solution)/shard_map/ppermute | solution.py:45
  372.6 21.7 %collective-permute-start.73 = (bf16[4,56,800]{2,1,0:T(8,128)(2,1)}, bf16[4,56,800]{2,1,0:T(8,128)(2,1)S(1)}, u32[]{:S(2)}, u32[]{:S(2)}) collective-permute-start(bf16[4,56,800]{2,1,0:T(8,128)(2,1)} %get-tuple-element.264), channel_id=1, source_target_pairs={{0,4},{4,0},{64,68},{68,64},{1,5},{5,1},{65,69},{69,65},{2,6},{6,2... | collective-permute-start | bytes 1075208 | tf_op jit(solution)/shard_map/ppermute | solution.py:45
  373.3 21.0 %collective-permute-start.74 = (bf16[3,56,800]{2,1,0:T(8,128)(2,1)}, bf16[3,56,800]{2,1,0:T(8,128)(2,1)S(1)}, u32[]{:S(2)}, u32[]{:S(2)}) collective-permute-start(bf16[3,56,800]{2,1,0:T(8,128)(2,1)} %get-tuple-element.270), channel_id=1, source_target_pairs={{0,68},{4,64},{64,4},{68,0},{1,69},{5,65},{65,5},{69,1},{2,70},{6,... | collective-permute-start | bytes 806408 | tf_op jit(solution)/shard_map/ppermute | solution.py:45
  401.6 18.8 %collective-permute-start.77 = (bf16[7,56,800]{2,1,0:T(8,128)(2,1)S(1)}, bf16[7,56,800]{2,1,0:T(8,128)(2,1)S(1)}, u32[]{:S(2)}, u32[]{:S(2)}) collective-permute-start(bf16[7,56,800]{2,1,0:T(8,128)(2,1)S(1)} %qkv_half.1.half), channel_id=1, source_target_pairs={{0,64},{4,68},{64,0},{68,4},{1,65},{5,69},{65,1},{69,5},{2,66},{6,... | collective-permute-start | bytes 1881608 | tf_op jit(solution)/shard_map/ppermute | solution.py:45
  407.3 17.0 %collective-permute-start.78 = (bf16[128,1664]{1,0:T(8,128)(2,1)S(1)}, bf16[128,1664]{1,0:T(8,128)(2,1)S(1)}, u32[]{:S(2)}, u32[]{:S(2)}) collective-permute-start(bf16[128,1664]{1,0:T(8,128)(2,1)S(1)} %get-tuple-element.309), channel_id=1, source_target_pairs={{0,1},{1,0},{2,3},{3,2},{4,5},{5,4},{6,7},{7,6},{8,9},{9,8},{10,11... | collective-permute-start | bytes 1277960 | tf_op jit(solution)/shard_map/ppermute | solution.py:37
  408.1 17.0 %collective-permute-start.79 = (bf16[128,1664]{1,0:T(8,128)(2,1)S(1)}, bf16[128,1664]{1,0:T(8,128)(2,1)S(1)}, u32[]{:S(2)}, u32[]{:S(2)}) collective-permute-start(bf16[128,1664]{1,0:T(8,128)(2,1)S(1)} %get-tuple-element.307), channel_id=1, source_target_pairs={{0,3},{1,2},{2,1},{3,0},{4,7},{5,6},{6,5},{7,4},{8,11},{9,10},{10,... | collective-permute-start | bytes 1277960 | tf_op jit(solution)/shard_map/ppermute | solution.py:37
  410.0 19.1 %collective-permute-start.80 = (bf16[128,1664]{1,0:T(8,128)(2,1)S(1)}, bf16[128,1664]{1,0:T(8,128)(2,1)S(1)}, u32[]{:S(2)}, u32[]{:S(2)}) collective-permute-start(bf16[128,1664]{1,0:T(8,128)(2,1)S(1)} %get-tuple-element.308), channel_id=1, source_target_pairs={{0,2},{1,3},{2,0},{3,1},{4,6},{5,7},{6,4},{7,5},{8,10},{9,11},{10,... | collective-permute-start | bytes 1277960 | tf_op jit(solution)/shard_map/ppermute | solution.py:37
  458.2 19.9 %collective-permute-start.87 = (bf16[7,56,800]{2,1,0:T(8,128)(2,1)S(1)}, bf16[7,56,800]{2,1,0:T(8,128)(2,1)S(1)}, u32[]{:S(2)}, u32[]{:S(2)}) collective-permute-start(bf16[7,56,800]{2,1,0:T(8,128)(2,1)S(1)} %qkv_z.1.refs_0_), channel_id=1, source_target_pairs={{0,32},{16,48},{32,0},{48,16},{1,33},{17,49},{33,1},{49,17},{2,34}... | collective-permute-start | bytes 1881608 | tf_op jit(solution)/shard_map/ppermute | solution.py:41
  (146 other events, 1506.5 us)
Sparse Core Ops, SparseCore 0:
  246.4 68.7 reduce-scatter.4
  332.8 22.2 reduce-scatter.2
  396.7 44.4 all-gather.2
where the time goes:
time: 508 us; the launch traced here: 498 us
  Pallas kernels  164 us (32%)
  starting transfers between devices  139 us (27%)
  waiting for transfers between devices  136 us (27%)
  local copies, waits for them, and re-layouts  29.3 us (6%)
  between operations  15.1 us (3%)
  other arithmetic  14 us (3%)
    ppermute x42, waiting for transfers between devices, z_swap(): return lax.ppermute(value, 'z', [(i, i ^ step) for i in range(4)])  71.4 us
    ppermute x42, starting transfers between devices, z_swap(): return lax.ppermute(value, 'z', [(i, i ^ step) for i in range(4)])  54.2 us
    ppermute x30, starting transfers between devices, c_swap(): return lax.ppermute(value, 'c', [(0, 1), (1, 0)])  53.2 us
    pallas_call x12, Pallas kernels, whole_call(): pl.pallas_call(body, in_specs=[SMEM] + [VMEM] * (len(args) - 1), out_spec...  35.1 us
    ppermute x12, waiting for transfers between devices, y_swap(): return lax.ppermute(value, ('yh', 'yl'), [(i, i ^ step) for i in range(4)])  27.5 us
    ppermute x6, waiting for transfers between devices, x_swap(): return lax.ppermute(value, 'x', [(i, i ^ step) for i in range(4)])  24 us
    pallas_call x1, Pallas kernels, feed(): pl.pallas_call(feed_kernel, grid=(rows // Q_ROWS,), in_specs=[SMEM, pl.Bl...  23.9 us
    unnamed x192, local copies, waits for them, and re-layouts  20 us
  transfers between devices with their start and end apart: 99, of which 40 were waited for; matrix products, arithmetic and copies ran while one was open for 4% of the time, Pallas kernels for 27%

commit v1 on v0

--- a/solution.py
+++ b/solution.py
@@ -568,24 +568,56 @@
         far[:, WIDTH:] = jnp.zeros((value.shape[0], LANES - WIDTH), LOW)
 
 
-def feed_kernel(at, bias, *refs):
-    cot_refs, normed_refs, fc_refs, proj_refs = refs[:8], refs[8:16], refs[16:20], refs[20:23]
-    hidden, d_in, near, far, bias_sum, normed, cot, fc, proj, wide, blocks, tall, back, *sems = (
-        refs[23:]
-    )
+def hidden_back_kernel(at, *refs):
+    cot_refs, proj_refs, (d_hidden, cot, proj, *sems) = refs[:8], refs[8:11], refs[11:]
+    step = pl.program_id(0)
+
+    def cot_copy(k):
+        return pltpu.make_async_copy(cot_refs[k], cot.at[k], sems[0].at[k])
+
+    @pl.when(step == 0)
+    def _():
+        for k in range(8):
+            cot_copy(k).start()
+        load_proj(at, proj_refs, proj, sems[1])
+
+    for k in range(8):
+
+        @pl.when(step == k // 2)
+        def _():
+            cot_copy(k).wait()
+
+    rows = cot[pl.ds(step * 2, 2)].reshape(2 * ROWS, WIDTH)
+    d_hidden[...] = lax.dot_general(rows, proj[...], ACROSS, preferred_element_type=WIDE)
+
+
+def hidden_back(at, cot, proj):
+    rows = 8 * ROWS
+    return pl.pallas_call(
+        hidden_back_kernel,
+        grid=(rows // Q_ROWS,),
+        in_specs=[SMEM] + [ANY] * 11,
+        out_specs=pl.BlockSpec((Q_ROWS, FF_PART), lambda i: (i, 0)),
+        out_shape=like((rows, FF_PART), WIDE),
+        scratch_shapes=[
+            pltpu.VMEM((8, ROWS, WIDTH), LOW),
+            pltpu.VMEM((FF_PART, WIDTH), LOW),
+            pltpu.SemaphoreType.DMA((8,)),
+            pltpu.SemaphoreType.DMA((2,)),
+        ],
+        compiler_params=pltpu.CompilerParams(vmem_limit_bytes=VMEM_LIMIT),
+        cost_estimate=cost(0),
+        name="hidden_back",
+    )(at, *cot, *proj)
+
+
+def feed_kernel(at, bias, d_hidden, *refs):
+    normed_refs, fc_refs, refs = refs[:8], refs[8:12], refs[12:]
+    hidden, d_in, near, far, bias_sum, normed, fc, wide, blocks, tall, back, *sems = refs
     step = pl.program_id(0)
 
     def normed_copy(k):
         return pltpu.make_async_copy(normed_refs[k], normed.at[k], sems[0].at[k])
-
-    def cot_copy(k):
-        return pltpu.make_async_copy(cot_refs[k], cot.at[k], sems[3].at[k])
-
-    own, got = proj_pairs(*proj_refs, proj)
-    diagonal = at[CORE] == at[YL]
-
-    def proj_copy(i):
-        return pltpu.make_async_copy(got[i][0], got[i][1], sems[2].at[i])
 
     @pl.when(step == 0)
     def _():
@@ -597,16 +629,6 @@
         wide[:, WIDTH:] = jnp.zeros((2 * ROWS, wide.shape[1] - WIDTH), LOW)
         for copy in copies:
             copy.wait()
-        for k in range(2):
-            cot_copy(k).start()
-
-        @pl.when(diagonal)
-        def _():
-            load(own, sems[2])
-
-        @pl.when(jnp.logical_not(diagonal))
-        def _():
-            load(got, sems[2])
 
     for k in range(8):
 
@@ -617,7 +639,6 @@
         @pl.when(step + 1 == k // 2)
         def _():
             normed_copy(k).start()
-            cot_copy(k).start()
 
     wide[:, :WIDTH] = normed[pl.ds(step * 2, 2)].reshape(2 * ROWS, WIDTH)
 
@@ -627,26 +648,13 @@
     to_blocks(wide, at[ME], write)
     weight = fc[...].reshape(8 * BLOCK, FF_PART)
     u = jnp.dot(blocks[...], weight, preferred_element_type=WIDE) + bias[...]
-    for k in range(8):
-
-        @pl.when(step == k // 2)
-        def _():
-            cot_copy(k).wait()
-
-    @pl.when(step == 0)
-    def _():
-        proj_copy(0).wait()
-        proj_copy(1).wait()
-
-    cot_rows = cot[pl.ds(step * 2, 2)].reshape(2 * ROWS, WIDTH)
-    d_hidden = lax.dot_general(cot_rows, proj[...], ACROSS, preferred_element_type=WIDE)
     factor = (2.0 / jnp.pi) ** 0.5
     square = u * u
     bent = jnp.tanh(factor * (u + 0.044715 * (square * u)))
     half = 0.5 * (1.0 + bent)
     hidden[...] = (u * half).astype(LOW)
     slope = half + (0.5 * factor) * u * (1.0 - bent * bent) * (1.0 + (3 * 0.044715) * square)
-    low = (d_hidden * slope).astype(LOW)
+    low = (d_hidden[...] * slope).astype(LOW)
     d_in[...] = low
     bias_sum[...] += jnp.sum(low.astype(WIDE), axis=0, keepdims=True)
     tall[...] = lax.dot_general(low, weight, ACROSS, preferred_element_type=WIDE).astype(LOW)
@@ -654,14 +662,19 @@
     write_half(step, near, far, back[...])
 
 
-def feed(at, normed, cot, fc, proj, bias):
+def feed(at, normed, d_hidden, fc, bias):
     rows = 8 * ROWS
     still = lambda i: (0, 0)
     down = lambda i: (i, 0)
     return pl.pallas_call(
         feed_kernel,
         grid=(rows // Q_ROWS,),
-        in_specs=[SMEM, pl.BlockSpec((1, FF_PART), still)] + [ANY] * 23,
+        in_specs=[
+            SMEM,
+            pl.BlockSpec((1, FF_PART), still),
+            pl.BlockSpec((Q_ROWS, FF_PART), down),
+        ]
+        + [ANY] * 12,
         out_specs=[
             pl.BlockSpec((Q_ROWS, FF_PART), down),
             pl.BlockSpec((Q_ROWS, FF_PART), down),
@@ -678,22 +691,18 @@
         ],
         scratch_shapes=[
             pltpu.VMEM((8, ROWS, WIDTH), LOW),
-            pltpu.VMEM((8, ROWS, WIDTH), LOW),
             pltpu.VMEM((8, BLOCK, FF_PART), LOW),
-            pltpu.VMEM((FF_PART, WIDTH), LOW),
             pltpu.VMEM((Q_ROWS, WIDTH + 192), LOW),
             pltpu.VMEM((Q_ROWS, 8 * BLOCK), LOW),
             pltpu.VMEM((Q_ROWS, 8 * BLOCK), LOW),
             pltpu.VMEM((Q_ROWS, WIDTH), LOW),
             pltpu.SemaphoreType.DMA((8,)),
             pltpu.SemaphoreType.DMA((8,)),
-            pltpu.SemaphoreType.DMA((2,)),
-            pltpu.SemaphoreType.DMA((8,)),
         ],
         compiler_params=pltpu.CompilerParams(vmem_limit_bytes=VMEM_LIMIT),
         cost_estimate=cost(0),
         name="feed_forward_and_back",
-    )(at, bias, *cot, *normed, *fc, *proj)
+    )(at, bias, d_hidden, *normed, *fc)
 
 
 def final_kernel(at, hidden, *refs):
@@ -1297,11 +1306,12 @@
         + OUT_WEIGHT_SCRATCH,
     )
 
-    all_second, second_came = gather_rows(normed_second)
+    d_hidden = hidden_back(at, after(all_cotangent, normed_second), proj_pieces)
+    all_second, second_came = gather_rows(normed_second, late=(d_hidden,))
     weight_fc = far_blocks(fc_near, normed_second)
     mixed_other = c_swap(after(mixed, second_came))
     hidden, d_hidden_in, d_second_near, d_second_far, fc_bias_sum = feed(
-        at, all_second, all_cotangent, weight_fc, proj_pieces, fc_bias_own
+        at, all_second, d_hidden, weight_fc, fc_bias_own
     )
     d_second_parts, d_second_sent, d_second_came = team_parts(d_second_near, d_second_far)
 

time: 508 us -> 503 us (level)
  waiting for transfers between devices: 136 us -> 128 us
  Pallas kernels: 164 us -> 170 us
    pallas_call x0 -> x1, Pallas kernels: none -> 9.16 us  [hidden_back(): pl.pallas_call(hidden_back_kernel, grid=(rows // Q_ROWS,), in_specs=[SMEM...]
    ppermute x42, waiting for transfers between devices: 71.4 us -> 63 us  [z_swap(): return lax.ppermute(value, 'z', [(i, i ^ step) for i in range(4)])]
    unnamed x192 -> x182, local copies, waits for them, and re-layouts: 20 us -> 19 us
  transfers between devices with their start and end apart: 99 -> 99, of which waited for: 40 -> 41; matrix products, arithmetic and copies ran while one was open for 4% -> 4% of each run, Pallas kernels for 27% -> 29%
where the time goes in v1:
time: 503 us; the launch traced here: 493 us
  Pallas kernels  170 us (34%)
  starting transfers between devices  138 us (27%)
  waiting for transfers between devices  128 us (25%)
  local copies, waits for them, and re-layouts  28.2 us (6%)
  between operations  15.1 us (3%)
  other arithmetic  14 us (3%)
    ppermute x42, waiting for transfers between devices, z_swap(): return lax.ppermute(value, 'z', [(i, i ^ step) for i in range(4)])  63 us
    ppermute x42, starting transfers between devices, z_swap(): return lax.ppermute(value, 'z', [(i, i ^ step) for i in range(4)])  54.2 us
    ppermute x30, starting transfers between devices, c_swap(): return lax.ppermute(value, 'c', [(0, 1), (1, 0)])  52 us
    pallas_call x12, Pallas kernels, whole_call(): pl.pallas_call(body, in_specs=[SMEM] + [VMEM] * (len(args) - 1), out_spec...  35.1 us
    ppermute x12, waiting for transfers between devices, y_swap(): return lax.ppermute(value, ('yh', 'yl'), [(i, i ^ step) for i in range(4)])  26.8 us
    ppermute x6, waiting for transfers between devices, x_swap(): return lax.ppermute(value, 'x', [(i, i ^ step) for i in range(4)])  24 us
    pallas_call x1, Pallas kernels, feed(): pl.pallas_call(feed_kernel, grid=(rows // Q_ROWS,), in_specs=[SMEM, pl.Bl...  20.3 us
    unnamed x182, local copies, waits for them, and re-layouts  19 us
  transfers between devices with their start and end apart: 99, of which 41 were waited for; matrix products, arithmetic and copies ran while one was open for 4% of the time, Pallas kernels for 29%

profile of v1, /device:TPU:27, one launch (start us, length us, event | category | flops | bytes accessed | tf_op | source)
XLA Modules:
  0.0 493.0 jit_solution(18079912862130684207)
XLA Ops:
  11.5 4.1 prepare_qkv.1
  15.7 3.4 collective-permute-start.9
  22.2 3.4 fusion
  34.0 13.8 %collective-permute-start.11 = (s32[1,4]{1,0:T(1,128)S(1)}, s32[1,4]{1,0:T(1,128)S(1)}, u32[]{:S(2)}, u32[]{:S(2)}) collective-permute-start(s32[1,4]{1,0:T(1,128)S(1)} %copy-done.87), channel_id=1, source_target_pairs={{0,8},{8,0},{1,9},{9,1},{2,10},{10,2},{3,11},{11,3},{4,12},{12,4},... | collective-permute-start | bytes 56 | tf_op jit(solution)/shard_map/ppermute | solution.py:49
  51.1 4.6 collective-permute-start.7
  64.0 10.3 %collective-permute-done.12.refs_10_.refs_2_ = bf16[2,208,768]{2,1,0:T(8,128)(2,1)S(1)} collective-permute-done((bf16[2,208,768]{2,1,0:T(8,128)(2,1)S(1)}, bf16[2,208,768]{2,1,0:T(8,128)(2,1)S(1)}, u32[]{:S(2)}, u32[]{:S(2)}) %collective-permute-start.12) | collective-permute-done | bytes 639008 | tf_op jit(solution)/shard_map/ppermute | solution.py:45
  81.8 4.6 collective-permute-start.22
  90.0 12.4 %first_norm_qkv.1 = (bf16[1024,1600]{1,0:T(8,128)(2,1)}, bf16[1024,768]{1,0:T(8,128)(2,1)}, f32[8,1600]{1,0:T(8,128)}, f32[1,800]{1,0:T(1,128)}) custom-call(s32[6]{0:T(128)} %stack.81.at.at_ref, bf16[128,1600]{1,0:T(8,128)(2,1)} %copy-done.1, bf16[128,1600]{1,0:T(8,128)(2,1)} %collective-permute-done.1.refs_1_, ...), custom_call_target="tpu_custom_call" | custom-call | tf_op jit(solution)/shard_map/first_norm_qkv/pallas_call | solution.py:319
  102.4 4.2 collective-permute-done.19.refs_3_
  114.0 2.8 collective-permute-start.26
  117.9 9.1 %attend.1 = (bf16[1024,256]{1,0:T(8,128)(2,1)}, f32[1024,128]{1,0:T(8,128)}) custom-call(s32[6]{0:T(128)} %stack.81.at.at_ref, s32[1,4]{1,0:T(1,128)} %broadcast_select_fusion.lengths, bf16[1024,768]{1,0:T(8,128)(2,1)} %get-tuple-element.203.q_ref.k_ref.v_ref, bf16[1024,768]{1,0:T(8,128)(2,1)} %get-tuple-element.203.q_ref.k_ref.v_ref, ...), custom_call_target="tpu_custom_call" | custom-call | tf_op jit(solution)/shard_map/attend/pallas_call | solution.py:455
  127.0 5.9 %collective-permute-done.26 = bf16[208,800]{1,0:T(8,128)(2,1)S(1)} collective-permute-done((bf16[208,800]{1,0:T(8,128)(2,1)S(1)}, bf16[208,800]{1,0:T(8,128)(2,1)S(1)}, u32[]{:S(2)}, u32[]{:S(2)}) %collective-permute-start.26) | collective-permute-done | bytes 332832 | tf_op jit(solution)/shard_map/ppermute | solution.py:37
  154.8 7.0 %out_and_second_norm.1 = (f32[128,1600]{1,0:T(8,128)}, bf16[128,1600]{1,0:T(8,128)(2,1)}, bf16[128,1600]{1,0:T(8,128)(2,1)}) custom-call(s32[6]{0:T(128)} %stack.81.at.at_ref, bf16[128,1600]{1,0:T(8,128)(2,1)} %copy-done.1, f32[8,1600]{1,0:T(8,128)} %get-tuple-element.304.vectors.refs_1_, bf16[128,512]{1,0:T(8,128)(2,1)} %pad_maximum_fusion.7.refs_0_, ...), custom_call_target="tpu_custom_call" | custom-call | tf_op jit(solution)/shard_map/out_and_second_norm/pallas_call | solution.py:141
  162.2 2.9 collective-permute-start.41
  165.8 3.4 collective-permute-start.43
  172.1 9.2 %hidden_back.1.d_hidden = f32[1024,800]{1,0:T(8,128)} custom-call(s32[6]{0:T(128)} %stack.81.at.at_ref, bf16[128,1600]{1,0:T(8,128)(2,1)} %collective-permute-done.14.refs_0_.cot, bf16[128,1600]{1,0:T(8,128)(2,1)} %collective-permute-done.18.refs_1_, bf16[128,1600]{1,0:T(8,128)(2,1)} %collective-permute-done.20.refs_2_, ...), custom_call_target="tpu_custom_call" | custom-call | tf_op jit(solution)/shard_map/hidden_back/pallas_call | solution.py:596
  182.6 5.1 %collective-permute-start.44 = (bf16[128,1600]{1,0:T(8,128)(2,1)S(1)}, bf16[128,1600]{1,0:T(8,128)(2,1)S(1)}, u32[]{:S(2)}, u32[]{:S(2)}) collective-permute-start(bf16[128,1600]{1,0:T(8,128)(2,1)S(1)} %collective-permute-done.40.refs_1_.refs_9_), channel_id=1, source_target_pairs={{0,8},{8,0},{1,9},{9,1},{2,10},{10,2},{3,11},{11,3},{4,12},{12,4},... | collective-permute-start | bytes 1228808 | tf_op jit(solution)/shard_map/ppermute | solution.py:49
  191.3 20.3 %feed_forward_and_back.1 = (bf16[1024,800]{1,0:T(8,128)(2,1)}, bf16[1024,800]{1,0:T(8,128)(2,1)}, bf16[512,1664]{1,0:T(8,128)(2,1)}, bf16[512,1664]{1,0:T(8,128)(2,1)}, f32[1,800]{1,0:T(1,128)}) custom-call(s32[6]{0:T(128)} %stack.81.at.at_ref, f32[1,800]{1,0:T(1,128)} %get-tuple-element.221.bias, f32[1024,800]{1,0:T(8,128)} %hidden_back.1.d_hidden, ...), custom_call_target="tpu_custom_call" | custom-call | tf_op jit(solution)/shard_map/feed_forward_and_back/pallas_call | solution.py:669
  212.7 3.4 collective-permute-done.49.got
  219.3 3.5 collective-permute-start.51
  223.0 15.8 %feed_forward_grad.1 = bf16[64,56,800]{2,1,0:T(8,128)(2,1)} custom-call(s32[6]{0:T(128)} %stack.81.at.at_ref, bf16[1024,800]{1,0:T(8,128)(2,1)} %get-tuple-element.289.hidden, bf16[1024,800]{1,0:T(8,128)(2,1)} %get-tuple-element.245.d_in, bf16[128,1600]{1,0:T(8,128)(2,1)} %collective-permute-done.14.refs_0_.cot, ...), custom_call_target="tpu_custom_call" | custom-call | tf_op jit(solution)/shard_map/feed_forward_grad/pallas_call | solution.py:1000
  243.7 8.9 %second_norm_and_out_back.1 = (f32[128,1600]{1,0:T(8,128)}, bf16[128,1600]{1,0:T(8,128)(2,1)}, f32[8,1600]{1,0:T(8,128)}, bf16[128,512]{1,0:T(8,128)(2,1)}, bf16...) custom-call(s32[6]{0:T(128)} %stack.81.at.at_ref, ...), custom_call_target="tpu_custom_call" | custom-call | tf_op jit(solution)/shard_map/second_norm_and_out_back/pallas_call | solution.py:851
  252.6 2.8 collective-permute-start.55
  257.7 4.9 %collective-permute-done.53 = bf16[128,512]{1,0:T(8,128)(2,1)S(1)} collective-permute-done((bf16[128,512]{1,0:T(8,128)(2,1)}, bf16[128,512]{1,0:T(8,128)(2,1)S(1)}, u32[]{:S(2)}, u32[]{:S(2)}) %collective-permute-start.53) | collective-permute-done | bytes 131104 | tf_op jit(solution)/shard_map/ppermute | solution.py:37
  264.3 4.1 out_grad.1
  274.5 15.4 %attend_back.1.d_qkv = bf16[1024,768]{1,0:T(8,128)(2,1)} custom-call(s32[6]{0:T(128)} %stack.81.at.at_ref, s32[1,4]{1,0:T(1,128)} %broadcast_select_fusion.lengths, bf16[1024,768]{1,0:T(8,128)(2,1)} %get-tuple-element.203.q_ref.k_ref.v_ref, bf16[1024,768]{1,0:T(8,128)(2,1)} %get-tuple-element.203.q_ref.k_ref.v_ref, ...), custom_call_target="tpu_custom_call" | custom-call | tf_op jit(solution)/shard_map/attend_back/pallas_call | solution.py:476
  290.0 7.6 %qkv_grad.1 = (bf16[8,56,800]{2,1,0:T(8,128)(2,1)}, bf16[8,56,800]{2,1,0:T(8,128)(2,1)}, bf16[8,56,800]{2,1,0:T(8,128)(2,1)}, bf16[8,56,800]{2,1,0:T(8,128)(2,1)}) custom-call(s32[6]{0:T(128)} %stack.81.at.at_ref, bf16[1024,1600]{1,0:T(8,128)(2,1)} %get-tuple-element.219.normed, bf16[1024,768]{1,0:T(8,128)(2,1)} %attend_back.1.d_qkv), custom_call_target="tpu_custom_call" | custom-call | tf_op jit(solution)/shard_map/qkv_grad/pallas_call | solution.py:102
  301.0 10.4 %qkv_back.1 = (bf16[512,1664]{1,0:T(8,128)(2,1)}, bf16[512,1664]{1,0:T(8,128)(2,1)}, f32[1,768]{1,0:T(1,128)}) custom-call(s32[6]{0:T(128)} %stack.81.at.at_ref, bf16[1024,768]{1,0:T(8,128)(2,1)} %attend_back.1.d_qkv, bf16[2,208,768]{2,1,0:T(8,128)(2,1)} %copy-done.30, bf16[2,208,768]{2,1,0:T(8,128)(2,1)} %copy-done.31, bf16[2,208,768]{2,1,0:T(8,128)(2,1)} %copy-done.39, ...), custom_call_target="tpu_custom_call" | custom-call | tf_op jit(solution)/shard_map/qkv_back/pallas_call | solution.py:895
  311.4 6.0 %collective-permute-done.64.refs_3_ = bf16[208,1600]{1,0:T(8,128)(2,1)S(1)} collective-permute-done((bf16[208,1600]{1,0:T(8,128)(2,1)S(1)}, bf16[208,1600]{1,0:T(8,128)(2,1)S(1)}, u32[]{:S(2)}, u32[]{:S(2)}) %collective-permute-start.64) | collective-permute-done | bytes 665632 | tf_op jit(solution)/shard_map/ppermute | solution.py:37
  317.3 4.2 collective-permute-done.61.refs_1_
  324.0 4.1 out_sum.1
  338.1 3.8 collective-permute-done.67.refs_2_
  343.9 7.6 %collective-permute-done.68.refs_3_ = bf16[128,1664]{1,0:T(8,128)(2,1)S(1)} collective-permute-done((bf16[128,1664]{1,0:T(8,128)(2,1)}, bf16[128,1664]{1,0:T(8,128)(2,1)S(1)}, u32[]{:S(2)}, u32[]{:S(2)}) %collective-permute-start.68) | collective-permute-done | bytes 426016 | tf_op jit(solution)/shard_map/ppermute | solution.py:37
  359.2 4.8 collective-permute-done.63.refs_3_
  363.9 4.2 qkv_x.1
  369.6 5.3 %collective-permute-done.72.two = bf16[8,56,800]{2,1,0:T(8,128)(2,1)} collective-permute-done((bf16[8,56,800]{2,1,0:T(8,128)(2,1)}, bf16[8,56,800]{2,1,0:T(8,128)(2,1)}, u32[]{:S(2)}, u32[]{:S(2)}) %collective-permute-start.72) | collective-permute-done | bytes 716832 | tf_op jit(solution)/shard_map/ppermute | solution.py:45
  380.7 9.0 %feed_forward_out.1 = (bf16[512,1664]{1,0:T(8,128)(2,1)}, bf16[512,1664]{1,0:T(8,128)(2,1)}) custom-call(s32[6]{0:T(128)} %stack.81.at.at_ref, bf16[1024,800]{1,0:T(8,128)(2,1)} %get-tuple-element.289.hidden, bf16[800,1600]{1,0:T(8,128)(2,1)} %refs_0_.3, bf16[400,1600]{1,0:T(8,128)(2,1)} %copy-done.32, bf16[400,1600]{1,0:T(8,128)(2,1)} %collective-permute-done.22.refs_10_.refs_2_), custom_call_target="tpu_custom_call" | custom-call | tf_op jit(solution)/shard_map/feed_forward_out/pallas_call | solution.py:722
  392.0 5.0 %collective-permute-start.75 = (bf16[512,1664]{1,0:T(8,128)(2,1)}, bf16[512,1664]{1,0:T(8,128)(2,1)S(1)}, u32[]{:S(2)}, u32[]{:S(2)}) collective-permute-start(bf16[512,1664]{1,0:T(8,128)(2,1)} %get-tuple-element.294), channel_id=1, source_target_pairs={{0,8},{8,0},{1,9},{9,1},{2,10},{10,2},{3,11},{11,3},{4,12},{12,4},... | collective-permute-start | bytes 5111816 | tf_op jit(solution)/shard_map/ppermute | solution.py:49
  407.5 8.3 %collective-permute-done.77.last = bf16[7,56,800]{2,1,0:T(8,128)(2,1)S(1)} collective-permute-done((bf16[7,56,800]{2,1,0:T(8,128)(2,1)S(1)}, bf16[7,56,800]{2,1,0:T(8,128)(2,1)S(1)}, u32[]{:S(2)}, u32[]{:S(2)}) %collective-permute-start.77) | collective-permute-done | bytes 627232 | tf_op jit(solution)/shard_map/ppermute | solution.py:45
  416.6 3.1 collective-permute-start.82
  420.5 4.1 collective-permute-done.80.refs_6_
  424.6 2.8 collective-permute-done.81.one
  427.4 5.9 %collective-permute-done.82.two = bf16[2,56,800]{2,1,0:T(8,128)(2,1)S(1)} collective-permute-done((bf16[2,56,800]{2,1,0:T(8,128)(2,1)S(1)}, bf16[2,56,800]{2,1,0:T(8,128)(2,1)S(1)}, u32[]{:S(2)}, u32[]{:S(2)}) %collective-permute-start.82) | collective-permute-done | bytes 179232 | tf_op jit(solution)/shard_map/ppermute | solution.py:37
  436.3 12.9 %collective-permute-done.85.refs_1_ = bf16[7,56,800]{2,1,0:T(8,128)(2,1)S(1)} collective-permute-done((bf16[7,56,800]{2,1,0:T(8,128)(2,1)S(1)}, bf16[7,56,800]{2,1,0:T(8,128)(2,1)S(1)}, u32[]{:S(2)}, u32[]{:S(2)}) %collective-permute-start.85) | collective-permute-done | bytes 627232 | tf_op jit(solution)/shard_map/ppermute | solution.py:41
  450.4 3.2 collective-permute-start.91
  456.3 3.7 output_rows.1
  461.8 8.1 %place_feed.1 = (f32[200,6400]{1,0:T(8,128)}, f32[800,1600]{1,0:T(8,128)}) custom-call(s32[6]{0:T(128)} %stack.81.at.at_ref, bf16[4,8,56,800]{3,2,1,0:T(8,128)(2,1)} %bitcast.25, bf16[4,8,56,800]{3,2,1,0:T(8,128)(2,1)} %collective-permute-done.91.other), custom_call_target="tpu_custom_call" | custom-call | tf_op jit(solution)/shard_map/place_feed/pallas_call | solution.py:102
  479.1 6.4 %place_qkv.1 = (f32[200,4800]{1,0:T(8,128)}, f32[200,1600]{1,0:T(8,128)}, f32[200]{0:T(256)}, f32[200]{0:T(256)}, f32[200]{0:T(256)}, /*index=5*/f32[200]{0:T(25...) custom-call(s32[6]{0:T(128)} %stack.81.at.at_ref, ...), custom_call_target="tpu_custom_call" | custom-call | tf_op jit(solution)/shard_map/place_qkv/pallas_call | solution.py:102
  (390 shorter events, 162.6 us)
Async XLA Ops:
  7.2 322.2 %reduce-scatter.5.cloned.1.call-start = ((), (), s32[]{:S(2)}) async-start(), calls=%async_computation.3 | async-start | bytes 8028160 | tf_op jit(solution)/shard_map/reduce_scatter | solution.py:1320
  15.6 16.9 %collective-permute-start.8 = (bf16[208,768]{1,0:T(8,128)(2,1)}, bf16[208,768]{1,0:T(8,128)(2,1)}, u32[]{:S(2)}, u32[]{:S(2)}) collective-permute-start(bf16[208,768]{1,0:T(8,128)(2,1)} %get-tuple-element.176), channel_id=1, source_target_pairs={{0,1},{1,0},{2,3},{3,2},{4,5},{5,4},{6,7},{7,6},{8,9},{9,8},{10,11... | collective-permute-start | bytes 958472 | tf_op jit(solution)/shard_map/ppermute | solution.py:37
  15.7 18.3 %collective-permute-start.9 = (bf16[208,768]{1,0:T(8,128)(2,1)}, bf16[208,768]{1,0:T(8,128)(2,1)}, u32[]{:S(2)}, u32[]{:S(2)}) collective-permute-start(bf16[208,768]{1,0:T(8,128)(2,1)} %get-tuple-element.177), channel_id=1, source_target_pairs={{0,2},{1,3},{2,0},{3,1},{4,6},{5,7},{6,4},{7,5},{8,10},{9,11},{10,... | collective-permute-start | bytes 958472 | tf_op jit(solution)/shard_map/ppermute | solution.py:37
  19.1 30.3 %collective-permute-start.10 = (bf16[208,768]{1,0:T(8,128)(2,1)}, bf16[208,768]{1,0:T(8,128)(2,1)}, u32[]{:S(2)}, u32[]{:S(2)}) collective-permute-start(bf16[208,768]{1,0:T(8,128)(2,1)} %get-tuple-element.178), channel_id=1, source_target_pairs={{0,3},{1,2},{2,1},{3,0},{4,7},{5,6},{6,5},{7,4},{8,11},{9,10},{10,... | collective-permute-start | bytes 958472 | tf_op jit(solution)/shard_map/ppermute | solution.py:37
  19.5 31.6 %collective-permute-start.2 = (bf16[128,1600]{1,0:T(8,128)(2,1)S(1)}, bf16[128,1600]{1,0:T(8,128)(2,1)}, u32[]{:S(2)}, u32[]{:S(2)}) collective-permute-start(bf16[128,1600]{1,0:T(8,128)(2,1)S(1)} %collective-permute-done.refs_0_.tokens), channel_id=1, source_target_pairs={{0,2},{1,3},{2,0},{3,1},{4,6},{5,7},{6,4},{7,5},{8,10},{9,11},{10,... | collective-permute-start | bytes 1228808 | tf_op jit(solution)/shard_map/ppermute | solution.py:37
  21.6 29.5 %collective-permute-start.3 = (bf16[128,1600]{1,0:T(8,128)(2,1)S(1)}, bf16[128,1600]{1,0:T(8,128)(2,1)}, u32[]{:S(2)}, u32[]{:S(2)}) collective-permute-start(bf16[128,1600]{1,0:T(8,128)(2,1)S(1)} %collective-permute-done.refs_0_.tokens), channel_id=1, source_target_pairs={{0,3},{1,2},{2,1},{3,0},{4,7},{5,6},{6,5},{7,4},{8,11},{9,10},{10,... | collective-permute-start | bytes 1228808 | tf_op jit(solution)/shard_map/ppermute | solution.py:37
  32.4 27.6 %collective-permute-start.14 = (bf16[128,1600]{1,0:T(8,128)(2,1)S(1)}, bf16[128,1600]{1,0:T(8,128)(2,1)}, u32[]{:S(2)}, u32[]{:S(2)}) collective-permute-start(bf16[128,1600]{1,0:T(8,128)(2,1)S(1)} %copy.34), channel_id=1, source_target_pairs={{0,0},{4,8},{8,4},{12,12},{1,1},{5,9},{9,5},{13,13},{2,2},{6,10},{... | collective-permute-start | bytes 1228808 | tf_op jit(solution)/shard_map/ppermute | solution.py:57
  60.2 17.6 %collective-permute-start.16 = (bf16[208,800]{1,0:T(8,128)(2,1)S(1)}, bf16[208,800]{1,0:T(8,128)(2,1)S(1)}, u32[]{:S(2)}, u32[]{:S(2)}) collective-permute-start(bf16[208,800]{1,0:T(8,128)(2,1)S(1)} %copy-done.15), channel_id=1, source_target_pairs={{0,2},{1,3},{2,0},{3,1},{4,6},{5,7},{6,4},{7,5},{8,10},{9,11},{10,... | collective-permute-start | bytes 998408 | tf_op jit(solution)/shard_map/ppermute | solution.py:37
  61.8 18.0 %collective-permute-start.17 = (bf16[208,800]{1,0:T(8,128)(2,1)S(1)}, bf16[208,800]{1,0:T(8,128)(2,1)S(1)}, u32[]{:S(2)}, u32[]{:S(2)}) collective-permute-start(bf16[208,800]{1,0:T(8,128)(2,1)S(1)} %copy-done.15), channel_id=1, source_target_pairs={{0,3},{1,2},{2,1},{3,0},{4,7},{5,6},{6,5},{7,4},{8,11},{9,10},{10,... | collective-permute-start | bytes 998408 | tf_op jit(solution)/shard_map/ppermute | solution.py:37
  79.8 28.4 %collective-permute-start.21 = (bf16[400,1600]{1,0:T(8,128)(2,1)}, bf16[400,1600]{1,0:T(8,128)(2,1)S(1)}, u32[]{:S(2)}, u32[]{:S(2)}) collective-permute-start(bf16[400,1600]{1,0:T(8,128)(2,1)} %get-tuple-element.201), channel_id=1, source_target_pairs={{0,4},{12,8},{64,68},{76,72},{1,5},{13,9},{65,69},{77,73},{2,6},{1... | collective-permute-start | bytes 3840008 | tf_op jit(solution)/shard_map/ppermute | solution.py:68
  81.8 26.3 %collective-permute-start.22 = (bf16[400,1600]{1,0:T(8,128)(2,1)}, bf16[400,1600]{1,0:T(8,128)(2,1)}, u32[]{:S(2)}, u32[]{:S(2)}) collective-permute-start(bf16[400,1600]{1,0:T(8,128)(2,1)} %get-tuple-element.202), channel_id=1, source_target_pairs={{0,68},{12,72},{64,4},{76,8},{1,69},{13,73},{65,5},{77,9},{2,70},{... | collective-permute-start | bytes 3840008 | tf_op jit(solution)/shard_map/ppermute | solution.py:68
  86.4 20.2 %collective-permute-start.19 = (bf16[128,1600]{1,0:T(8,128)(2,1)}, bf16[128,1600]{1,0:T(8,128)(2,1)}, u32[]{:S(2)}, u32[]{:S(2)}) collective-permute-start(bf16[128,1600]{1,0:T(8,128)(2,1)} %collective-permute-done.14.refs_0_.cot), channel_id=1, source_target_pairs={{0,3},{1,2},{2,1},{3,0},{4,7},{5,6},{6,5},{7,4},{8,11},{9,10},{10,... | collective-permute-start | bytes 1228808 | tf_op jit(solution)/shard_map/ppermute | solution.py:37
  88.8 19.4 %collective-permute-start.20 = (bf16[128,1600]{1,0:T(8,128)(2,1)}, bf16[128,1600]{1,0:T(8,128)(2,1)}, u32[]{:S(2)}, u32[]{:S(2)}) collective-permute-start(bf16[128,1600]{1,0:T(8,128)(2,1)} %collective-permute-done.14.refs_0_.cot), channel_id=1, source_target_pairs={{0,2},{1,3},{2,0},{3,1},{4,6},{5,7},{6,4},{7,5},{8,10},{9,11},{10,... | collective-permute-start | bytes 1228808 | tf_op jit(solution)/shard_map/ppermute | solution.py:37
  110.4 24.6 %collective-permute-start.23 = (bf16[2,208,800]{2,1,0:T(8,128)(2,1)S(1)}, bf16[2,208,800]{2,1,0:T(8,128)(2,1)}, u32[]{:S(2)}, u32[]{:S(2)}) collective-permute-start(bf16[2,208,800]{2,1,0:T(8,128)(2,1)S(1)} %pad_maximum_fusion.refs_4_.refs_3_), channel_id=1, source_target_pairs={{0,4},{4,0},{64,68},{68,64},{1,5},{5,1},{65,69},{69,65},{2,6},{6,2... | collective-permute-start | bytes 1996808 | tf_op jit(solution)/shard_map/ppermute | solution.py:45
  111.7 23.2 %collective-permute-start.24 = (bf16[2,208,800]{2,1,0:T(8,128)(2,1)S(1)}, bf16[2,208,800]{2,1,0:T(8,128)(2,1)}, u32[]{:S(2)}, u32[]{:S(2)}) collective-permute-start(bf16[2,208,800]{2,1,0:T(8,128)(2,1)S(1)} %pad_maximum_fusion.1.refs_5_.refs_4_), channel_id=1, source_target_pairs={{0,68},{4,64},{64,4},{68,0},{1,69},{5,65},{65,5},{69,1},{2,70},{6,... | collective-permute-start | bytes 1996808 | tf_op jit(solution)/shard_map/ppermute | solution.py:45
  114.0 18.8 %collective-permute-start.26 = (bf16[208,800]{1,0:T(8,128)(2,1)S(1)}, bf16[208,800]{1,0:T(8,128)(2,1)S(1)}, u32[]{:S(2)}, u32[]{:S(2)}) collective-permute-start(bf16[208,800]{1,0:T(8,128)(2,1)S(1)} %copy-done.25), channel_id=1, source_target_pairs={{0,2},{1,3},{2,0},{3,1},{4,6},{5,7},{6,4},{7,5},{8,10},{9,11},{10,... | collective-permute-start | bytes 998408 | tf_op jit(solution)/shard_map/ppermute | solution.py:37
  116.8 18.2 %collective-permute-start.27 = (bf16[208,800]{1,0:T(8,128)(2,1)S(1)}, bf16[208,800]{1,0:T(8,128)(2,1)}, u32[]{:S(2)}, u32[]{:S(2)}) collective-permute-start(bf16[208,800]{1,0:T(8,128)(2,1)S(1)} %copy-done.23), channel_id=1, source_target_pairs={{0,3},{1,2},{2,1},{3,0},{4,7},{5,6},{6,5},{7,4},{8,11},{9,10},{10,... | collective-permute-start | bytes 998408 | tf_op jit(solution)/shard_map/ppermute | solution.py:37
  142.0 20.1 %collective-permute-start.36 = (bf16[128,1600]{1,0:T(8,128)(2,1)}, bf16[128,1600]{1,0:T(8,128)(2,1)S(1)}, u32[]{:S(2)}, u32[]{:S(2)}) collective-permute-start(bf16[128,1600]{1,0:T(8,128)(2,1)} %collective-permute-done.14.refs_0_.cot), channel_id=1, source_target_pairs={{0,8},{8,0},{1,9},{9,1},{2,10},{10,2},{3,11},{11,3},{4,12},{12,4},... | collective-permute-start | bytes 1228808 | tf_op jit(solution)/shard_map/ppermute | solution.py:49
  142.4 22.6 %collective-permute-start.37 = (bf16[128,1600]{1,0:T(8,128)(2,1)}, bf16[128,1600]{1,0:T(8,128)(2,1)S(1)}, u32[]{:S(2)}, u32[]{:S(2)}) collective-permute-start(bf16[128,1600]{1,0:T(8,128)(2,1)} %collective-permute-done.18.refs_1_), channel_id=1, source_target_pairs={{0,8},{8,0},{1,9},{9,1},{2,10},{10,2},{3,11},{11,3},{4,12},{12,4},... | collective-permute-start | bytes 1228808 | tf_op jit(solution)/shard_map/ppermute | solution.py:49
  143.5 22.2 %collective-permute-start.38 = (bf16[128,1600]{1,0:T(8,128)(2,1)}, bf16[128,1600]{1,0:T(8,128)(2,1)S(1)}, u32[]{:S(2)}, u32[]{:S(2)}) collective-permute-start(bf16[128,1600]{1,0:T(8,128)(2,1)} %collective-permute-done.20.refs_2_), channel_id=1, source_target_pairs={{0,8},{8,0},{1,9},{9,1},{2,10},{10,2},{3,11},{11,3},{4,12},{12,4},... | collective-permute-start | bytes 1228808 | tf_op jit(solution)/shard_map/ppermute | solution.py:49
  152.4 18.2 %collective-permute-start.39 = (bf16[128,1600]{1,0:T(8,128)(2,1)}, bf16[128,1600]{1,0:T(8,128)(2,1)S(1)}, u32[]{:S(2)}, u32[]{:S(2)}) collective-permute-start(bf16[128,1600]{1,0:T(8,128)(2,1)} %collective-permute-done.19.refs_3_), channel_id=1, source_target_pairs={{0,8},{8,0},{1,9},{9,1},{2,10},{10,2},{3,11},{11,3},{4,12},{12,4},... | collective-permute-start | bytes 1228808 | tf_op jit(solution)/shard_map/ppermute | solution.py:49
  162.2 20.4 %collective-permute-start.41 = (bf16[128,1600]{1,0:T(8,128)(2,1)}, bf16[128,1600]{1,0:T(8,128)(2,1)}, u32[]{:S(2)}, u32[]{:S(2)}) collective-permute-start(bf16[128,1600]{1,0:T(8,128)(2,1)} %get-tuple-element.225.refs_0_.refs_8_), channel_id=1, source_target_pairs={{0,2},{1,3},{2,0},{3,1},{4,6},{5,7},{6,4},{7,5},{8,10},{9,11},{10,... | collective-permute-start | bytes 1228808 | tf_op jit(solution)/shard_map/ppermute | solution.py:37
  165.0 22.7 %collective-permute-start.42 = (bf16[128,1600]{1,0:T(8,128)(2,1)}, bf16[128,1600]{1,0:T(8,128)(2,1)}, u32[]{:S(2)}, u32[]{:S(2)}) collective-permute-start(bf16[128,1600]{1,0:T(8,128)(2,1)} %get-tuple-element.225.refs_0_.refs_8_), channel_id=1, source_target_pairs={{0,3},{1,2},{2,1},{3,0},{4,7},{5,6},{6,5},{7,4},{8,11},{9,10},{10,... | collective-permute-start | bytes 1228808 | tf_op jit(solution)/shard_map/ppermute | solution.py:37
  165.8 22.1 %collective-permute-start.43 = (bf16[128,1600]{1,0:T(8,128)(2,1)}, bf16[128,1600]{1,0:T(8,128)(2,1)}, u32[]{:S(2)}, u32[]{:S(2)}) collective-permute-start(bf16[128,1600]{1,0:T(8,128)(2,1)} %get-tuple-element.225.refs_0_.refs_8_), channel_id=1, source_target_pairs={{0,8},{8,0},{1,9},{9,1},{2,10},{10,2},{3,11},{11,3},{4,12},{12,4},... | collective-permute-start | bytes 1228808 | tf_op jit(solution)/shard_map/ppermute | solution.py:49
  170.6 18.5 %collective-permute-start.47 = (bf16[2,208,800]{2,1,0:T(8,128)(2,1)S(1)}, bf16[2,208,800]{2,1,0:T(8,128)(2,1)}, u32[]{:S(2)}, u32[]{:S(2)}) collective-permute-start(bf16[2,208,800]{2,1,0:T(8,128)(2,1)S(1)} %pad_maximum_fusion.2.refs_8_), channel_id=1, source_target_pairs={{0,4},{4,0},{64,68},{68,64},{1,5},{5,1},{65,69},{69,65},{2,6},{6,2... | collective-permute-start | bytes 1996808 | tf_op jit(solution)/shard_map/ppermute | solution.py:45
  170.9 18.2 %collective-permute-start.48 = (bf16[2,208,800]{2,1,0:T(8,128)(2,1)S(1)}, bf16[2,208,800]{2,1,0:T(8,128)(2,1)}, u32[]{:S(2)}, u32[]{:S(2)}) collective-permute-start(bf16[2,208,800]{2,1,0:T(8,128)(2,1)S(1)} %pad_maximum_fusion.3.refs_9_), channel_id=1, source_target_pairs={{0,68},{4,64},{64,4},{68,0},{1,69},{5,65},{65,5},{69,1},{2,70},{6,... | collective-permute-start | bytes 1996808 | tf_op jit(solution)/shard_map/ppermute | solution.py:45
  218.4 20.5 %collective-permute-start.50 = (bf16[128,1664]{1,0:T(8,128)(2,1)S(1)}, bf16[128,1664]{1,0:T(8,128)(2,1)S(1)}, u32[]{:S(2)}, u32[]{:S(2)}) collective-permute-start(bf16[128,1664]{1,0:T(8,128)(2,1)S(1)} %get-tuple-element.337), channel_id=1, source_target_pairs={{0,1},{1,0},{2,3},{3,2},{4,5},{5,4},{6,7},{7,6},{8,9},{9,8},{10,11... | collective-permute-start | bytes 1277960 | tf_op jit(solution)/shard_map/ppermute | solution.py:37
  219.3 21.2 %collective-permute-start.51 = (bf16[128,1664]{1,0:T(8,128)(2,1)S(1)}, bf16[128,1664]{1,0:T(8,128)(2,1)S(1)}, u32[]{:S(2)}, u32[]{:S(2)}) collective-permute-start(bf16[128,1664]{1,0:T(8,128)(2,1)S(1)} %get-tuple-element.335), channel_id=1, source_target_pairs={{0,3},{1,2},{2,1},{3,0},{4,7},{5,6},{6,5},{7,4},{8,11},{9,10},{10,... | collective-permute-start | bytes 1277960 | tf_op jit(solution)/shard_map/ppermute | solution.py:37
  222.9 18.7 %collective-permute-start.52 = (bf16[128,1664]{1,0:T(8,128)(2,1)S(1)}, bf16[128,1664]{1,0:T(8,128)(2,1)S(1)}, u32[]{:S(2)}, u32[]{:S(2)}) collective-permute-start(bf16[128,1664]{1,0:T(8,128)(2,1)S(1)} %get-tuple-element.336), channel_id=1, source_target_pairs={{0,2},{1,3},{2,0},{3,1},{4,6},{5,7},{6,4},{7,5},{8,10},{9,11},{10,... | collective-permute-start | bytes 1277960 | tf_op jit(solution)/shard_map/ppermute | solution.py:37
  242.3 121.6 %reduce-scatter.3.cloned.1.call-start = ((), (), s32[]{:S(2)}) async-start(), calls=%async_computation.2 | async-start | bytes 1003520 | tf_op jit(solution)/shard_map/reduce_scatter | solution.py:1375
  242.3 20.4 %collective-permute-start.56 = (bf16[128,1600]{1,0:T(8,128)(2,1)S(1)}, bf16[128,1600]{1,0:T(8,128)(2,1)S(1)}, u32[]{:S(2)}, u32[]{:S(2)}) collective-permute-start(bf16[128,1600]{1,0:T(8,128)(2,1)S(1)} %copy-done.65), channel_id=1, source_target_pairs={{0,8},{8,0},{1,9},{9,1},{2,10},{10,2},{3,11},{11,3},{4,12},{12,4},... | collective-permute-start | bytes 1228808 | tf_op jit(solution)/shard_map/ppermute | solution.py:49
  268.4 21.5 %collective-permute-start.59 = (bf16[208,1600]{1,0:T(8,128)(2,1)}, bf16[208,1600]{1,0:T(8,128)(2,1)S(1)}, u32[]{:S(2)}, u32[]{:S(2)}) collective-permute-start(bf16[208,1600]{1,0:T(8,128)(2,1)} %get-tuple-element.259), channel_id=1, source_target_pairs={{0,1},{1,0},{2,3},{3,2},{4,5},{5,4},{6,7},{7,6},{8,9},{9,8},{10,11... | collective-permute-start | bytes 1996808 | tf_op jit(solution)/shard_map/ppermute | solution.py:37
  269.4 20.5 %collective-permute-start.60 = (bf16[208,1600]{1,0:T(8,128)(2,1)}, bf16[208,1600]{1,0:T(8,128)(2,1)S(1)}, u32[]{:S(2)}, u32[]{:S(2)}) collective-permute-start(bf16[208,1600]{1,0:T(8,128)(2,1)} %get-tuple-element.260), channel_id=1, source_target_pairs={{0,3},{1,2},{2,1},{3,0},{4,7},{5,6},{6,5},{7,4},{8,11},{9,10},{10,... | collective-permute-start | bytes 1996808 | tf_op jit(solution)/shard_map/ppermute | solution.py:37
  297.5 24.0 %collective-permute-start.61 = (bf16[8,56,800]{2,1,0:T(8,128)(2,1)}, bf16[8,56,800]{2,1,0:T(8,128)(2,1)S(1)}, u32[]{:S(2)}, u32[]{:S(2)}) collective-permute-start(bf16[8,56,800]{2,1,0:T(8,128)(2,1)} %get-tuple-element.263), channel_id=1, source_target_pairs={{0,16},{16,0},{32,48},{48,32},{1,17},{17,1},{33,49},{49,33},{2,18}... | collective-permute-start | bytes 2150408 | tf_op jit(solution)/shard_map/ppermute | solution.py:41
  298.0 24.5 %collective-permute-start.62 = (bf16[8,56,800]{2,1,0:T(8,128)(2,1)}, bf16[8,56,800]{2,1,0:T(8,128)(2,1)S(1)}, u32[]{:S(2)}, u32[]{:S(2)}) collective-permute-start(bf16[8,56,800]{2,1,0:T(8,128)(2,1)} %get-tuple-element.264), channel_id=1, source_target_pairs={{0,48},{16,32},{32,16},{48,0},{1,49},{17,33},{33,17},{49,1},{2,50}... | collective-permute-start | bytes 2150408 | tf_op jit(solution)/shard_map/ppermute | solution.py:41
  299.7 17.6 %collective-permute-start.64 = (bf16[208,1600]{1,0:T(8,128)(2,1)S(1)}, bf16[208,1600]{1,0:T(8,128)(2,1)S(1)}, u32[]{:S(2)}, u32[]{:S(2)}) collective-permute-start(bf16[208,1600]{1,0:T(8,128)(2,1)S(1)} %copy-done.89), channel_id=1, source_target_pairs={{0,2},{1,3},{2,0},{3,1},{4,6},{5,7},{6,4},{7,5},{8,10},{9,11},{10,... | collective-permute-start | bytes 1996808 | tf_op jit(solution)/shard_map/ppermute | solution.py:37
  328.1 122.4 %all-gather.3.cloned.1.call-start = ((), (), s32[]{:S(2)}) async-start(), calls=%async_computation.4 | async-start | bytes 4014080 | tf_op jit(solution)/shard_map/all_gather | solution.py:1420
  331.9 19.6 %collective-permute-start.68 = (bf16[128,1664]{1,0:T(8,128)(2,1)}, bf16[128,1664]{1,0:T(8,128)(2,1)S(1)}, u32[]{:S(2)}, u32[]{:S(2)}) collective-permute-start(bf16[128,1664]{1,0:T(8,128)(2,1)} %get-tuple-element.332), channel_id=1, source_target_pairs={{0,3},{1,2},{2,1},{3,0},{4,7},{5,6},{6,5},{7,4},{8,11},{9,10},{10,... | collective-permute-start | bytes 1277960 | tf_op jit(solution)/shard_map/ppermute | solution.py:37
  333.8 19.6 %collective-permute-start.69 = (bf16[128,1664]{1,0:T(8,128)(2,1)}, bf16[128,1664]{1,0:T(8,128)(2,1)S(1)}, u32[]{:S(2)}, u32[]{:S(2)}) collective-permute-start(bf16[128,1664]{1,0:T(8,128)(2,1)} %get-tuple-element.333), channel_id=1, source_target_pairs={{0,2},{1,3},{2,0},{3,1},{4,6},{5,7},{6,4},{7,5},{8,10},{9,11},{10,... | collective-permute-start | bytes 1277960 | tf_op jit(solution)/shard_map/ppermute | solution.py:37
  341.9 22.0 %collective-permute-start.63 = (bf16[8,56,800]{2,1,0:T(8,128)(2,1)S(1)}, bf16[8,56,800]{2,1,0:T(8,128)(2,1)}, u32[]{:S(2)}, u32[]{:S(2)}) collective-permute-start(bf16[8,56,800]{2,1,0:T(8,128)(2,1)S(1)} %copy-done.88), channel_id=1, source_target_pairs={{0,32},{16,48},{32,0},{48,16},{1,33},{17,49},{33,1},{49,17},{2,34}... | collective-permute-start | bytes 2150408 | tf_op jit(solution)/shard_map/ppermute | solution.py:41
  355.0 19.9 %collective-permute-start.72 = (bf16[8,56,800]{2,1,0:T(8,128)(2,1)}, bf16[8,56,800]{2,1,0:T(8,128)(2,1)}, u32[]{:S(2)}, u32[]{:S(2)}) collective-permute-start(bf16[8,56,800]{2,1,0:T(8,128)(2,1)} %feed_half.1.one), channel_id=1, source_target_pairs={{0,64},{4,68},{64,0},{68,4},{1,65},{5,69},{65,1},{69,5},{2,66},{6,... | collective-permute-start | bytes 2150408 | tf_op jit(solution)/shard_map/ppermute | solution.py:45
  368.1 21.6 %collective-permute-start.73 = (bf16[4,56,800]{2,1,0:T(8,128)(2,1)}, bf16[4,56,800]{2,1,0:T(8,128)(2,1)S(1)}, u32[]{:S(2)}, u32[]{:S(2)}) collective-permute-start(bf16[4,56,800]{2,1,0:T(8,128)(2,1)} %get-tuple-element.286), channel_id=1, source_target_pairs={{0,4},{4,0},{64,68},{68,64},{1,5},{5,1},{65,69},{69,65},{2,6},{6,2... | collective-permute-start | bytes 1075208 | tf_op jit(solution)/shard_map/ppermute | solution.py:45
  368.8 20.9 %collective-permute-start.74 = (bf16[3,56,800]{2,1,0:T(8,128)(2,1)}, bf16[3,56,800]{2,1,0:T(8,128)(2,1)S(1)}, u32[]{:S(2)}, u32[]{:S(2)}) collective-permute-start(bf16[3,56,800]{2,1,0:T(8,128)(2,1)} %get-tuple-element.292), channel_id=1, source_target_pairs={{0,68},{4,64},{64,4},{68,0},{1,69},{5,65},{65,5},{69,1},{2,70},{6,... | collective-permute-start | bytes 806408 | tf_op jit(solution)/shard_map/ppermute | solution.py:45
  397.0 18.8 %collective-permute-start.77 = (bf16[7,56,800]{2,1,0:T(8,128)(2,1)S(1)}, bf16[7,56,800]{2,1,0:T(8,128)(2,1)S(1)}, u32[]{:S(2)}, u32[]{:S(2)}) collective-permute-start(bf16[7,56,800]{2,1,0:T(8,128)(2,1)S(1)} %qkv_half.1.half), channel_id=1, source_target_pairs={{0,64},{4,68},{64,0},{68,4},{1,65},{5,69},{65,1},{69,5},{2,66},{6,... | collective-permute-start | bytes 1881608 | tf_op jit(solution)/shard_map/ppermute | solution.py:45
  402.7 17.0 %collective-permute-start.78 = (bf16[128,1664]{1,0:T(8,128)(2,1)S(1)}, bf16[128,1664]{1,0:T(8,128)(2,1)S(1)}, u32[]{:S(2)}, u32[]{:S(2)}) collective-permute-start(bf16[128,1664]{1,0:T(8,128)(2,1)S(1)} %get-tuple-element.331), channel_id=1, source_target_pairs={{0,1},{1,0},{2,3},{3,2},{4,5},{5,4},{6,7},{7,6},{8,9},{9,8},{10,11... | collective-permute-start | bytes 1277960 | tf_op jit(solution)/shard_map/ppermute | solution.py:37
  403.5 17.0 %collective-permute-start.79 = (bf16[128,1664]{1,0:T(8,128)(2,1)S(1)}, bf16[128,1664]{1,0:T(8,128)(2,1)S(1)}, u32[]{:S(2)}, u32[]{:S(2)}) collective-permute-start(bf16[128,1664]{1,0:T(8,128)(2,1)S(1)} %get-tuple-element.329), channel_id=1, source_target_pairs={{0,3},{1,2},{2,1},{3,0},{4,7},{5,6},{6,5},{7,4},{8,11},{9,10},{10,... | collective-permute-start | bytes 1277960 | tf_op jit(solution)/shard_map/ppermute | solution.py:37
  405.4 19.1 %collective-permute-start.80 = (bf16[128,1664]{1,0:T(8,128)(2,1)S(1)}, bf16[128,1664]{1,0:T(8,128)(2,1)S(1)}, u32[]{:S(2)}, u32[]{:S(2)}) collective-permute-start(bf16[128,1664]{1,0:T(8,128)(2,1)S(1)} %get-tuple-element.330), channel_id=1, source_target_pairs={{0,2},{1,3},{2,0},{3,1},{4,6},{5,7},{6,4},{7,5},{8,10},{9,11},{10,... | collective-permute-start | bytes 1277960 | tf_op jit(solution)/shard_map/ppermute | solution.py:37
  453.6 19.8 %collective-permute-start.87 = (bf16[7,56,800]{2,1,0:T(8,128)(2,1)S(1)}, bf16[7,56,800]{2,1,0:T(8,128)(2,1)S(1)}, u32[]{:S(2)}, u32[]{:S(2)}) collective-permute-start(bf16[7,56,800]{2,1,0:T(8,128)(2,1)S(1)} %qkv_z.1.refs_0_), channel_id=1, source_target_pairs={{0,32},{16,48},{32,0},{48,16},{1,33},{17,49},{33,1},{49,17},{2,34}... | collective-permute-start | bytes 1881608 | tf_op jit(solution)/shard_map/ppermute | solution.py:41
  (141 other events, 1381.2 us)
Sparse Core Ops, SparseCore 0:
  241.7 68.8 reduce-scatter.4
  328.2 22.3 reduce-scatter.2
  392.1 44.4 all-gather.2
